TPU v7x, 256 devices: a whole 4x4x8 slice. The times are simulated.
256 devices in a mesh: ctx: 16 (over z, x_lo), head: 8 (over y, x_hi), rep: 2 (over core).
Axes of the slice: x: 4 (x_hi: 2, x_lo: 2; x = x_hi * 2 + x_lo), y: 4, z: 8, core: 2. Of those that a mesh axis runs over, the one named last changes fastest.
Arguments:
- queries: bfloat16 [2, 4096, 4096], P('rep', 'ctx', 'head'), may hold values from -1.1953125 to 1.1953125
- key_vecs: bfloat16 [2, 4096, 4096], P('rep', 'ctx', 'head'), may hold values from -1.1953125 to 1.1953125
- values: bfloat16 [2, 4096, 4096], P('rep', 'ctx', 'head'), may hold values from -6 to 6
- out_grad: bfloat16 [2, 4096, 4096], P('rep', 'ctx', 'head'), may hold values from -6 to 6
- out_weight: bfloat16 [4096, 4096], P('head', 'ctx'), may hold values from -0.09375 to 0.09375
- sign_bits: int32 [32, 3, 256], P('head'), may hold values from 0 to 1
Outputs:
- query_grad: bfloat16 [2, 4096, 4096], P('rep', 'ctx', 'head')
- key_grad: bfloat16 [2, 4096, 4096], P('rep', 'ctx', 'head')
- value_grad: bfloat16 [2, 4096, 4096], P('rep', 'ctx', 'head')
- out_weight_grad: bfloat16 [4096, 4096], P('head', 'ctx')
Inputs may be any that keep to these rules, and one draw needn't show every extreme that they name: `sign_bits`: each entry is a bit; the sign it gives is 2 bit - 1.
All inputs are finite; a program needn't handle non-finite values.
Results may differ from a plain program's by a relative error of at most 0.0095.
Values may be sent and summed in bfloat16 or wider, within the bound.
A program may use at most 128 MiB of HBM per device.

v0:
```python
import math

import jax
import jax.numpy as jnp
from jax import lax
from jax.sharding import PartitionSpec as P

DH = 128
M = 256
GROUP = 256


TOP_PRECISION = lax.Precision.HIGHEST


def prefix(value, axis, join, neutral, backward):
    count, mine = (lax.axis_size(axis), lax.axis_index(axis))
    pieces = jax.tree.map(lambda part: lax.all_gather(part, axis), value)
    if backward:
        pieces = jax.tree.map(lambda part: part[::-1], pieces)
        mine = count - 1 - mine
    subtotal = jax.tree.map(
        lambda part, zero: jnp.full_like(part, 0) + jnp.asarray(zero, part.dtype), value, neutral
    )

    def step(position, subtotal):
        longer = join(subtotal, jax.tree.map(lambda part: part[position], pieces))
        return jax.tree.map(lambda new, old: jnp.where(position < mine, new, old), longer, subtotal)

    return lax.fori_loop(0, count - 1, step, subtotal)


def hadamard_table(order):
    row_index = jnp.arange(order, dtype=jnp.int32)[:, None]
    col_index = jnp.arange(order, dtype=jnp.int32)[None, :]
    common = jnp.bitwise_and(row_index, col_index)
    parity = jnp.zeros((order, order), jnp.int32)
    for place in range(order.bit_length()):
        parity = parity + jnp.bitwise_and(jnp.right_shift(common, place), 1)
    return (1 - 2 * (parity % 2)).astype(jnp.float32)


def sign_matrix(bits):
    signs = 2.0 * bits.astype(jnp.float32) - 1.0
    hadam = hadamard_table(DH)
    blocks = []
    for block in range(M // DH):
        piece = signs[:, block * DH : (block + 1) * DH]
        mixing_matrix = hadam * piece[2][None, :]
        mixing_matrix = jnp.dot(hadam, piece[1][:, None] * mixing_matrix, precision=TOP_PRECISION)
        mixing_matrix = jnp.dot(hadam, piece[0][:, None] * mixing_matrix, precision=TOP_PRECISION)
        blocks.append(mixing_matrix / DH)
    return jnp.concatenate(blocks, axis=0)


def feature_map(rows, mixing_matrices):
    rescaled_rows = rows.astype(jnp.float32) * DH ** (-0.25)
    random_projection = jnp.einsum(
        "seu,exu->sex", rescaled_rows, mixing_matrices, precision=TOP_PRECISION
    )
    feats = jnp.exp(
        random_projection - 0.5 * jnp.sum(rescaled_rows * rescaled_rows, axis=-1, keepdims=True)
    ) / math.sqrt(M)
    return (rescaled_rows, feats)


def feature_back(grad_feat, rescaled_rows, feats, mixing_matrices):
    weighted_rows = grad_feat * feats
    backward_fn = jnp.einsum(
        "epv,pvk->epk", weighted_rows, mixing_matrices, precision=TOP_PRECISION
    ) - rescaled_rows * jnp.sum(weighted_rows, axis=-1, keepdims=True)
    return (DH ** (-0.25) * backward_fn).astype(jnp.bfloat16)


def bmix(form, left, right):
    return jnp.einsum(form, left, right, preferred_element_type=jnp.float32)


def fmix(form, left, right):
    return jnp.einsum(
        form, left, right, precision=TOP_PRECISION, preferred_element_type=jnp.float32
    )


def add_pair(first, second):
    return (first[0] + second[0], first[1] + second[1])


def on_device(queries, key_vecs, values, out_grad, out_weight, sign_bits):
    tokens = queries.shape[1]
    head_dev = queries.shape[2] // DH
    nchunk = tokens // GROUP
    mixing_matrices = jax.vmap(sign_matrix)(sign_bits)
    full_grad = lax.all_gather(out_grad, "head", axis=2, tiled=True).reshape(tokens, -1)
    cols = full_grad
    head_grad = bmix("tc,rc->tr", cols, lax.all_gather(out_weight, "ctx", axis=1, tiled=True))
    q_scaled, q_feat = feature_map(queries.reshape(tokens, head_dev, DH), mixing_matrices)
    k_scaled, k_feat = feature_map(key_vecs.reshape(tokens, head_dev, DH), mixing_matrices)
    qf = q_feat.astype(jnp.bfloat16).reshape(nchunk, GROUP, head_dev, M)
    kf = k_feat.astype(jnp.bfloat16).reshape(nchunk, GROUP, head_dev, M)
    vals = values.reshape(nchunk, GROUP, head_dev, DH)
    causal = jnp.arange(GROUP)[:, None] >= jnp.arange(GROUP)[None, :]
    causal_masked = jnp.where(causal, bmix("nthm,nshm->nhts", qf, kf), 0.0)
    masked_b = causal_masked.astype(jnp.bfloat16)
    group_kv = bmix("nshm,nshd->nhmd", kf, vals)
    group_kz = jnp.sum(kf, axis=1, dtype=jnp.float32)
    dev_kv = jnp.sum(group_kv, axis=0)
    dev_kz = jnp.sum(group_kz, axis=0)
    empty_pair = (jnp.zeros_like(dev_kv), jnp.zeros_like(dev_kz))
    kv_in, kz_in = prefix((dev_kv, dev_kz), "ctx", add_pair, empty_pair, False)
    kv_prev = kv_in[None] + jnp.cumsum(group_kv, axis=0) - group_kv
    kz_prev = kz_in[None] + jnp.cumsum(group_kz, axis=0) - group_kz
    kv_prev_b = kv_prev.astype(jnp.bfloat16)
    numer = bmix("nhts,nshd->nthd", masked_b, vals) + bmix("nthm,nhmd->nthd", qf, kv_prev_b)
    denom = jnp.swapaxes(jnp.sum(causal_masked, axis=-1), 1, 2) + fmix("nthm,nhm->nth", qf, kz_prev)
    attn = numer / denom[..., None]
    attn_b = attn.astype(jnp.bfloat16)
    grad_o = head_grad.reshape(nchunk, GROUP, head_dev, DH)
    grad_num_b = (grad_o / denom[..., None]).astype(jnp.bfloat16)
    grad_den = -jnp.sum(grad_o * attn, axis=-1) / denom
    group_rq = bmix("nthm,nthd->nhmd", qf, grad_num_b)
    group_rz = fmix("nthm,nth->nhm", qf, grad_den)
    dev_rq = jnp.sum(group_rq, axis=0)
    dev_rz = jnp.sum(group_rz, axis=0)
    rq_in, rz_in = prefix(
        (dev_rq, dev_rz), "ctx", add_pair, (jnp.zeros_like(dev_rq), jnp.zeros_like(dev_rz)), True
    )
    rq_next = (rq_in + dev_rq)[None] - jnp.cumsum(group_rq, axis=0)
    rz_next = (rz_in + dev_rz)[None] - jnp.cumsum(group_rz, axis=0)
    rq_next_b = rq_next.astype(jnp.bfloat16)
    mixed = jnp.where(
        causal,
        bmix("nthd,nshd->nhts", grad_num_b, vals) + jnp.swapaxes(grad_den, 1, 2)[..., None],
        0.0,
    ).astype(jnp.bfloat16)
    grad_qf = (
        bmix("nhts,nshm->nthm", mixed, kf)
        + bmix("nthd,nhmd->nthm", grad_num_b, kv_prev_b)
        + grad_den[..., None] * kz_prev[:, None]
    )
    grad_kf = (
        bmix("nhts,nthm->nshm", mixed, qf)
        + bmix("nshd,nhmd->nshm", vals, rq_next_b)
        + rz_next[:, None]
    )
    grad_v = bmix("nhts,nthd->nshd", masked_b, grad_num_b) + bmix("nshm,nhmd->nshd", kf, rq_next_b)
    query_grad = feature_back(
        grad_qf.reshape(tokens, head_dev, M), q_scaled, q_feat, mixing_matrices
    ).reshape(1, tokens, -1)
    key_grad = feature_back(
        grad_kf.reshape(tokens, head_dev, M), k_scaled, k_feat, mixing_matrices
    ).reshape(1, tokens, -1)
    value_grad = grad_v.astype(jnp.bfloat16).reshape(1, tokens, -1)
    attn_flat = attn_b.reshape(tokens, head_dev * DH)
    cols = full_grad
    partial_rows = lax.psum_scatter(
        bmix("tc,tr->cr", cols, attn_flat), "ctx", scatter_dimension=0, tiled=True
    )
    summed = lax.psum(partial_rows, "rep")
    weight_out = summed.astype(jnp.bfloat16).T
    return (query_grad, key_grad, value_grad, weight_out)


def solution(mesh):
    in_specs = (
        P("rep", "ctx", "head"),
        P("rep", "ctx", "head"),
        P("rep", "ctx", "head"),
        P("rep", "ctx", "head"),
        P("head", "ctx"),
        P("head", None, None),
    )
    out_specs = (
        P("rep", "ctx", "head"),
        P("rep", "ctx", "head"),
        P("rep", "ctx", "head"),
        P("head", "ctx"),
    )
    return jax.shard_map(
        on_device, mesh=mesh, in_specs=in_specs, out_specs=out_specs, check_vma=False
    )
```

profile of v0, /device:TPU:1, one launch (start us, length us, event | category | flops | bytes accessed | tf_op | source)
XLA Modules:
  0.0 785.3 jit_solution(4557075059837099206)
XLA Ops:
  13.7 2.2 convert_reduce_fusion
  17.2 30.4 %all-gather.4 = f32[16,4,256]{2,1,0:T(4,128)S(1)} all-gather(f32[1,4,256]{2,1,0:T(4,128)S(1)} %bitcast.221), channel_id=3, replica_groups=mesh['ctx'=16,'head'=8,'rep'=2] {'ctx'}, dimensions={0}, use_global_device_ids=true | all-gather | bytes 69632 | tf_op jit(solution)/shard_map/all_gather | solution.py:18
  47.8 2.1 fusion.96
  51.0 22.4 %all-gather.11.cloned.1.call-done = bf16[1,256,4096]{2,1,0:T(8,128)(2,1)} async-done(((bf16[1,256,512]{2,1,0:T(8,128)(2,1)}), bf16[1,256,4096]{2,1,0:T(8,128)(2,1)}) %all-gather.11.cloned.1.call-update) | async-done | bytes 2097168 | tf_op jit(solution)/shard_map/all_gather | solution.py:94
  73.5 111.7 %all-gather.13.cloned.1.call-done = bf16[512,4096]{1,0:T(8,128)(2,1)} async-done(((bf16[512,256]{1,0:T(8,128)(2,1)}), bf16[512,4096]{1,0:T(8,128)(2,1)}) %all-gather.13.cloned.1.call-update) | async-done | bytes 4194320 | tf_op jit(solution)/shard_map/all_gather | solution.py:96
  185.2 4.9 fusion.1
  190.1 188.4 %all-gather.15.cloned.1.call-done = f32[64,256,128]{2,1,0:T(8,128)} async-done(((f32[4,256,128]{2,1,0:T(8,128)}), f32[64,256,128]{2,1,0:T(8,128)}) %all-gather.15.cloned.1.call-update) | async-done | bytes 8388624 | tf_op jit(solution)/shard_map/all_gather | solution.py:18
  378.5 19.0 %while.32 = (s32[]{:T(128)}, f32[4,256,128]{2,1,0:T(8,128)S(1)}, f32[4,256]{1,0:T(4,128)S(1)}, s32[]{:T(128)}, f32[16,4,256,128]{3,2,1,0:T(8,128)}, /*index=5*/f32[16,4,256]{2,1,0:T(4,128)S(1)}, s32[]{:T(128)}, s32[]{:T(128)}) while((s32[]{:T(128)}, f32[4,256,128]{2,1,0:T(8,128)S(1)}, f32[4,256]{1,0:T(4,128)S(1)}, s32[]{:T(128)}, ...), condition=%wide.region_5.6_spmd.clone, body=%wide.region_4.5_spmd.clone.sunk | while | flops 396292 | bytes 1585275 | solution.py:30
  378.5 1.3 add_select_fusion.9
  379.9 1.2 add_select_fusion.9
  381.1 1.2 add_select_fusion.9
  382.4 1.2 add_select_fusion.9
  401.9 1.6 fusion.95
  403.5 4.5 convolution_bitcast_fusion
  408.9 1.2 fusion.18
  410.2 1.4 fusion.101
  411.6 1.6 fusion.98
  413.2 1.8 fusion.26
  415.0 1.8 copy.69
  417.3 30.5 %all-gather.5 = f32[16,4,256]{2,1,0:T(4,128)S(1)} all-gather(f32[1,4,256]{2,1,0:T(4,128)S(1)} %bitcast.222), channel_id=5, replica_groups=mesh['ctx'=16,'head'=8,'rep'=2] {'ctx'}, dimensions={0}, use_global_device_ids=true | all-gather | bytes 69632 | tf_op jit(solution)/shard_map/all_gather | solution.py:18
  447.9 2.2 fusion.37
  450.0 135.9 %all-gather.17.cloned.1.call-done = f32[64,256,128]{2,1,0:T(8,128)} async-done(((f32[4,256,128]{2,1,0:T(8,128)}), f32[64,256,128]{2,1,0:T(8,128)}) %all-gather.17.cloned.1.call-update) | async-done | bytes 8388624 | tf_op jit(solution)/shard_map/all_gather | solution.py:18
  585.9 7.6 rev.6
  593.5 19.0 %while.33 = (s32[]{:T(128)}, f32[4,256,128]{2,1,0:T(8,128)S(1)}, f32[4,256]{1,0:T(4,128)S(1)}, s32[]{:T(128)}, f32[16,4,256,128]{3,2,1,0:T(8,128)}, /*index=5*/f32[16,4,256]{2,1,0:T(4,128)S(1)}, s32[]{:T(128)}, s32[]{:T(128)}) while((s32[]{:T(128)}, f32[4,256,128]{2,1,0:T(8,128)S(1)}, f32[4,256]{1,0:T(4,128)S(1)}, s32[]{:T(128)}, ...), condition=%wide.region_9.10_spmd.clone, body=%wide.region_8.9_spmd.clone.sunk | while | flops 396292 | bytes 1585275 | solution.py:30
  593.5 1.3 add_select_fusion.11
  599.9 1.2 add_select_fusion.11
  601.1 1.2 add_select_fusion.11
  607.5 1.2 add_select_fusion.11
  608.7 1.2 add_select_fusion.11
  613.3 1.8 fusion.99
  618.3 154.0 %reduce-scatter.2.cloned.1.call-done = f32[256,512]{0,1:T(8,128)} async-done(((f32[4096,512]{0,1:T(8,128)}), f32[256,512]{0,1:T(8,128)}) %reduce-scatter.2.cloned.1.call-update) | async-done | bytes 524304 | tf_op jit(solution)/shard_map/reduce_scatter | solution.py:156
  772.2 6.6 all-reduce.1
  (132 shorter events, 44.6 us)
Async XLA Ops:
  7.2 66.3 %all-gather.11.cloned.1.call-start = ((), (), s32[]{:S(2)}) async-start(), calls=%async_computation.1 | async-start | bytes 2359296 | tf_op jit(solution)/shard_map/all_gather | solution.py:94
  7.9 177.3 %all-gather.13.cloned.1.call-start = ((), (), s32[]{:S(2)}) async-start(), calls=%async_computation.2 | async-start | bytes 4456448 | tf_op jit(solution)/shard_map/all_gather | solution.py:96
  8.6 8.4 %copy-start.14 = (bf16[1,256,512]{2,1,0:T(8,128)(2,1)S(1)}, bf16[1,256,512]{2,1,0:T(8,128)(2,1)}, u32[]{:S(2)}) copy-start(bf16[1,256,512]{2,1,0:T(8,128)(2,1)} %param.10) | copy-start | bytes 786436
  8.7 369.9 %all-gather.15.cloned.1.call-start = ((), (), s32[]{:S(2)}) async-start(), calls=%async_computation.4 | async-start | bytes 8912896 | tf_op jit(solution)/shard_map/all_gather | solution.py:18
  10.8 36.9 %copy-start.7 = (bf16[256,4,128]{2,1,0:T(4,128)(2,1)}, bf16[256,4,128]{2,1,0:T(4,128)(2,1)S(1)}, u32[]{:S(2)}) copy-start(bf16[256,4,128]{2,1,0:T(4,128)(2,1)S(1)} %reshape.256) | copy-start | bytes 786436
  13.7 36.2 %copy-start.2 = (f32[4,128,128]{2,1,0:T(8,128)}, f32[4,128,128]{2,1,0:T(8,128)S(1)}, u32[]{:S(2)}) copy-start(f32[4,128,128]{2,1,0:T(8,128)S(1)} %fusion.29) | copy-start | bytes 786436
  17.0 568.9 %all-gather.17.cloned.1.call-start = ((), (), s32[]{:S(2)}) async-start(), calls=%async_computation.5 | async-start | bytes 8912896 | tf_op jit(solution)/shard_map/all_gather | solution.py:18
  378.5 22.3 %copy-start.1 = (f32[4,256,128]{2,1,0:T(8,128)S(1)}, f32[4,256,128]{2,1,0:T(8,128)}, u32[]{:S(2)}) copy-start(f32[4,256,128]{2,1,0:T(8,128)} %fusion.49) | copy-start | bytes 1572868
  398.9 0.7 copy-start.4
  400.8 371.5 %reduce-scatter.2.cloned.1.call-start = ((), (), s32[]{:S(2)}) async-start(), calls=%async_computation.3 | async-start | bytes 8912896 | tf_op jit(solution)/shard_map/reduce_scatter | solution.py:156
  400.8 2.7 copy-start.12
  400.9 0.7 copy-start.6
  408.0 0.9 copy-start.5
  408.0 5.2 copy-start.3
  410.2 4.9 copy-start.13
  593.5 19.1 %copy-start = (f32[4,256,128]{2,1,0:T(8,128)S(1)}, f32[4,256,128]{2,1,0:T(8,128)}, u32[]{:S(2)}) copy-start(f32[4,256,128]{2,1,0:T(8,128)} %fusion.102) | copy-start | bytes 1572868
  593.5 19.1 %copy-start.8 = (bf16[256,4,128]{2,1,0:T(4,128)(2,1)S(1)}, bf16[256,4,128]{2,1,0:T(4,128)(2,1)}, u32[]{:S(2)}) copy-start(bf16[256,4,128]{2,1,0:T(4,128)(2,1)} %copy-done.7) | copy-start | bytes 786436
  612.6 0.7 copy-start.9
  612.6 4.5 copy-start.11
  613.3 3.8 copy-start.10
Sparse Core Ops, SparseCore 0:
  10.5 62.9 all-gather.10
  75.2 109.9 all-gather.12
  187.0 191.4 all-gather.14
  400.9 184.9 all-gather.16
  588.3 183.8 reduce-scatter.1
where the time goes:
time: 787 us; the launch traced here: 785 us
  waiting for transfers between devices  614 us (78%)
  blocking collectives  67.6 us (9%)
  other arithmetic  39.4 us (5%)
  matrix products  33.3 us (4%)
  local copies, waits for them, and re-layouts  16.1 us (2%)
  between operations  14.2 us (2%)
    all_gather x2, waiting for transfers between devices, prefix(): pieces = jax.tree.map(lambda part: lax.all_gather(part, axis), value)  324 us
    reduce_scatter x1, waiting for transfers between devices, on_device(): lax.psum_scatter(bmix('tc,tr->cr', cols, attn_flat), 'ctx', scatter_dimen...  154 us
    all_gather x1, waiting for transfers between devices, on_device(): lax.all_gather(out_weight, 'ctx', axis=1, tiled=True)  112 us
    all_gather x2, blocking collectives, prefix(): pieces = jax.tree.map(lambda part: lax.all_gather(part, axis), value)  61 us
    select_n x60, other arithmetic, step(): jnp.where(position < mine, new, old)  37.2 us
    all_gather x1, waiting for transfers between devices, on_device(): lax.all_gather(out_grad, 'head', axis=2, tiled=True).reshape(tokens, -1)  22.4 us
    dot_general x13, matrix products, bmix(): return jnp.einsum(form, left, right, preferred_element_type=jnp.float32)  18.5 us
  transfers between devices with their start and end apart: 5, of which 5 were waited for; matrix products, arithmetic and copies ran while one was open for 8% of the time, Pallas kernels for 0%

commit v1 on v0

v1 whole, which is shorter than its diff:
```python
import functools

import jax
import jax.numpy as jnp
from jax import lax
from jax.experimental import pallas as pl
from jax.experimental.pallas import tpu as pltpu
from jax.sharding import PartitionSpec as P

DH = 128
M = 256
T = 256
HL = 4
NZ = 8
NC = 16
SL = 80
C = DH ** (-0.25)
F32 = jnp.float32
BF16 = jnp.bfloat16
MESH = pl.DeviceIdType.MESH

AX = 0
AYP, AYM, AYP2, AYM2 = 4, 8, 12, 14
AC = 16
BZP, BZM, BC = 20, 24, 27
GX, AT, CP, CM, CC = 34, 35, 38, 42, 45
D1A, D1B, D2A, D2B = 46, 62, 78, 94
NSEM = 110


def dot_nn(a, b):
    return lax.dot_general(a, b, (((1,), (0,)), ((), ())), preferred_element_type=F32)


def dot_nt(a, b):
    return lax.dot_general(a, b, (((1,), (1,)), ((), ())), preferred_element_type=F32)


def dot_tn(a, b):
    return lax.dot_general(a, b, (((0,), (0,)), ((), ())), preferred_element_type=F32)


def hadamard():
    i = lax.broadcasted_iota(jnp.int32, (DH, DH), 0)
    j = lax.broadcasted_iota(jnp.int32, (DH, DH), 1)
    x = i & j
    x = x ^ (x >> 4)
    x = x ^ (x >> 2)
    x = x ^ (x >> 1)
    return (1 - 2 * (x & 1)).astype(F32)


def head_cols(i):
    return pl.ds(pl.multiple_of(i * DH, DH), DH)


def kernel(q_ref, k_ref, v_ref, og_ref, ow_ref, sb_ref,
           qg_ref, kg_ref, vg_ref, wg_ref,
           ogg, owg, gacc, gsend, grecv,
           st, rv, po, pr, st2, rv2, po2, pr2,
           wc, pq, pk, qf, kf, ab, nv, rs, rd, attn, at, atg,
           gnb, gd, dk0, dv0, cps, cms, crp, crm,
           ssem, rsem):
    ctx = lax.axis_index("ctx")
    head = lax.axis_index("head")
    rep = lax.axis_index("rep")
    z, xl = ctx // 2, ctx % 2
    y, xh = head // 2, head % 2
    x = xh * 2 + xl
    sib = {"rep": 1 - rep}
    pair_ctx = z * 2 + 1 - xl
    pair = {"ctx": pair_ctx}
    pair_sib = {"ctx": pair_ctx, "rep": 1 - rep}
    yp = {"head": (head + 2) % 8}
    ym = {"head": (head + 6) % 8}
    zp = {"ctx": (ctx + 2) % NC}
    zm = {"ctx": (ctx + NC - 2) % NC}

    def xdev(k):
        xx = (x + k) % 4
        return {"ctx": z * 2 + xx % 2, "head": y * 2 + xx // 2}

    def rcopy(src, dst, n, dev):
        return pltpu.make_async_remote_copy(
            src_ref=src, dst_ref=dst, send_sem=ssem.at[n], recv_sem=rsem.at[n],
            device_id=dev, device_id_type=MESH)

    barrier = pltpu.get_barrier_semaphore()

    def greet(d, _):
        pl.semaphore_signal(barrier, inc=1, device_id={"ctx": (ctx + d) % NC}, device_id_type=MESH)
        return 0

    lax.fori_loop(1, NC, greet, 0)
    for dev in (sib, pair_sib, yp, ym):
        pl.semaphore_signal(barrier, inc=1, device_id=dev, device_id_type=MESH)
    for k in range(1, 4):
        xx = (x + k) % 4

        @pl.when(xx // 2 != xh)
        def _():
            pl.semaphore_signal(barrier, inc=1, device_id=xdev(k), device_id_type=MESH)

    hd = hadamard()
    hb = hd.astype(BF16)

    def mixing(i, _):
        bits = sb_ref[i].astype(F32) * 2.0 - 1.0
        for blk in range(2):
            s = bits[:, blk * DH:(blk + 1) * DH]
            inner = dot_nn((hd * s[1:2]).astype(BF16), hb).astype(BF16)
            w = dot_nn((hd * s[0:1]).astype(BF16), inner) * (s[2:3] * (1.0 / DH))
            hi = w.astype(BF16)
            lo = (w - hi.astype(F32)).astype(BF16)
            wc[i, blk * DH:(blk + 1) * DH, 0:DH] = hi
            wc[i, blk * DH:(blk + 1) * DH, DH:2 * DH] = lo
        return 0

    lax.fori_loop(0, HL, mixing, 0)

    pl.semaphore_wait(barrier, 21)

    def half(s):
        return og_ref.at[:, pl.ds(pl.multiple_of(s * 256, 256), 256)]

    my_b = head
    ax = []
    for k in range(1, 4):
        xx = (x + k) % 4
        c = rcopy(half(xx % 2), ogg.at[0, my_b, xl], AX + k, xdev(k))
        c.start()
        ax.append(c)

    rows_r = pl.ds(pl.multiple_of(rep * 256, 256), 256)

    bzp, bzm = [], []
    owg[z] = ow_ref[...]

    def z_send(s, up):
        blk = (z + NZ - s) % NZ if up else (z + s) % NZ
        ref = owg.at[blk, rows_r]
        c = rcopy(ref, ref, (BZP if up else BZM) + s, zp if up else zm)
        c.start()
        (bzp if up else bzm).append(c)

    z_send(0, True)
    z_send(0, False)

    def piece(yy, k):
        xx = (x + 4 - k) % 4
        return ogg.at[0, yy * 2 + xx // 2, xx % 2]

    sends = []
    ayp, aym = {}, {}

    def y_send(k):
        p = piece(y, k)
        ayp[k] = rcopy(p, p, AYP + k, yp)
        aym[k] = rcopy(p, p, AYM + k, ym)
        ayp[k].start()
        aym[k].start()

    ogg[0, my_b, xl] = og_ref[:, pl.ds(pl.multiple_of(xl * 256, 256), 256)]
    y_send(0)

    def features(x_ref, i):
        xb = x_ref[:, head_cols(i)]
        xf = xb.astype(F32)
        proj = dot_nt(jnp.concatenate([xb, xb], axis=1), wc[i]) * C
        norm = jnp.sum(xf * xf, axis=-1, keepdims=True) * (0.5 * C * C)
        return jnp.exp(proj - norm) * (1.0 / 16.0)

    def put_state(buf, i, s, zrow):
        zh = zrow.astype(BF16).astype(F32)
        zl = zrow - zh
        rowid = lax.broadcasted_iota(jnp.int32, (16, DH), 0)
        sb = s.astype(BF16)
        for t in range(4):
            g = slice((t // 2) * DH, (t // 2 + 1) * DH)
            buf[4 * i + t, 0:64, :] = sb[64 * t:64 * (t + 1)]
            buf[4 * i + t, 64:80, :] = jnp.where(
                rowid == 0, zh[:, g], jnp.where(rowid == 1, zl[:, g], 0.0)).astype(BF16)

    def get_state(buf, i):
        s = jnp.concatenate([buf[4 * i + t, 0:64, :] for t in range(4)], axis=0)
        za = buf[4 * i, 64:80, :].astype(F32)
        zb = buf[4 * i + 2, 64:80, :].astype(F32)
        zrow = jnp.concatenate([za[0:1] + za[1:2], zb[0:1] + zb[1:2]], axis=1)
        return s, zrow

    def k_phase(i, _):
        p = features(k_ref, i)
        pk[i] = p
        kb = p.astype(BF16)
        kf[i] = kb
        put_state(st, i, dot_tn(kb, v_ref[:, head_cols(i)]),
                  jnp.sum(kb.astype(F32), axis=0, keepdims=True))
        return 0

    lax.fori_loop(0, HL, k_phase, 0)

    def scan_copy(src, dst, n, d):
        to = (ctx + d) % NC
        return rcopy(src.at[to], dst.at[ctx], n + d, {"ctx": to})

    def scan_each(fn):
        lax.fori_loop(1, NC, lambda d, _: (fn(d), 0)[1], 0)

    def scan_send(src, dst, n):
        scan_each(lambda d: scan_copy(src, dst, n, d).start())

    def scan_recv(src, dst, n):
        scan_each(lambda d: scan_copy(src, dst, n, d).wait_recv())

    def scan_sent(src, dst, n):
        scan_each(lambda d: scan_copy(src, dst, n, d).wait_send())

    def running(rbuf, obuf, backward):
        rowid = lax.broadcasted_iota(jnp.int32, (16, DH), 0)

        def step(n, carry):
            cs, cz = carry
            c = NC - 1 - n if backward else n
            ch = cz.astype(BF16).astype(F32)
            cl = cz - ch
            obuf[c, 0:64, :] = cs.astype(BF16)
            obuf[c, 64:80, :] = jnp.where(
                rowid == 0, ch, jnp.where(rowid == 1, cl, 0.0)).astype(BF16)
            zin = rbuf[c, 64:80, :].astype(F32)
            return cs + rbuf[c, 0:64, :].astype(F32), cz + zin[0:1] + zin[1:2]

        lax.fori_loop(0, NC, step, (jnp.zeros((64, DH), F32), jnp.zeros((1, DH), F32)))

    scan_send(st, rv, D1A)

    for k in range(1, 4):
        ax[k - 1].wait_recv()
        y_send(k)

    bc = []

    def b_recv(s, up):
        (bzp if up else bzm)[s].wait_recv()
        blk = (z + NZ - 1 - s) % NZ if up else (z + 1 + s) % NZ
        ref = owg.at[blk, rows_r]
        if s + 1 < (4 if up else 3):
            z_send(s + 1, up)
        c = rcopy(ref, ref, BC + (s if up else 4 + s), sib)
        c.start()
        bc.append(c)

    ac = []

    def a_sib(n):
        yy = (y + n) % 4
        c = rcopy(ogg.at[0, pl.ds(yy * 2, 2)], ogg.at[1, pl.ds(yy * 2, 2)], AC + n, sib)
        c.start()
        ac.append(c)

    b_recv(0, True)
    b_recv(0, False)
    a_sib(0)

    tri = (lax.broadcasted_iota(jnp.int32, (T, T), 0)
           >= lax.broadcasted_iota(jnp.int32, (T, T), 1))

    def q_phase(i, _):
        p = features(q_ref, i)
        pq[i] = p
        qb = p.astype(BF16)
        qf[i] = qb
        am = jnp.where(tri, dot_nt(qb, kf[i]), 0.0)
        rs[i] = jnp.sum(am, axis=-1, keepdims=True)
        amb = am.astype(BF16)
        ab[i] = amb
        nv[i] = dot_nn(amb, v_ref[:, head_cols(i)])
        return 0

    lax.fori_loop(0, HL, q_phase, 0)

    b_recv(1, True)
    b_recv(1, False)

    scan_recv(st, rv, D1A)
    rv[ctx] = st[ctx]
    running(rv, po, False)
    pr[ctx] = po[ctx]
    scan_send(po, pr, D1B)

    b_recv(2, True)
    b_recv(2, False)

    ay2 = []
    for k in range(4):
        ayp[k].wait_recv()
        if k < 2:
            p = piece((y + 3) % 4, k)
            c = rcopy(p, p, AYP2 + k, yp)
            c.start()
            ay2.append(c)
        aym[k].wait_recv()
        if k >= 2:
            p = piece((y + 1) % 4, k)
            c = rcopy(p, p, AYM2 + k - 2, ym)
            c.start()
            ay2.append(c)
    b_recv(3, True)
    a_sib(3)
    a_sib(1)

    scan_recv(po, pr, D1B)

    def attn_phase(i, _):
        s, zrow = get_state(pr, i)
        qb = qf[i]
        den = rs[i] + jnp.sum(qb.astype(F32) * zrow, axis=-1, keepdims=True)
        r = 1.0 / den
        rd[i] = r
        a = (nv[i] + dot_nn(qb, s)) * r
        attn[i] = a
        at[i] = a.astype(BF16).T
        return 0

    lax.fori_loop(0, HL, attn_phase, 0)

    def at_half(n):
        return at.at[pl.ds(n * 2, 2)]

    atc = [rcopy(at_half(1 - rep), atg.at[1, xl], AT, sib),
           rcopy(at_half(rep), atg.at[0, xl], AT + 1, pair),
           rcopy(at_half(1 - rep), atg.at[1, xl], AT + 2, pair_sib)]
    for c in atc:
        c.start()
    atg[0, xl] = at[pl.ds(rep * 2, 2)]

    for c in bc:
        c.wait_recv()

    def go_group(n):
        yy = (y + n) % 4

        def tile(m, _):
            rows = pl.ds(pl.multiple_of(m % 2 * 128, 128), 128)
            acc = dot_nt(ogg[0, yy * 2, m // 2, rows, :], owg[yy * 2])
            acc += dot_nt(ogg[0, yy * 2 + 1, m // 2, rows, :], owg[yy * 2 + 1])
            if n == 0:
                gacc[m // 2, rows, :] = acc
            elif n == 2:
                total = gacc[m // 2, rows, :] + acc
                gacc[m // 2, rows, :] = total
                gsend[m // 2, rows, :] = total.astype(BF16)
            else:
                gacc[m // 2, rows, :] += acc
            return 0

        lax.fori_loop(0, 4, tile, 0)

    go_group(0)
    go_group(1)
    go_group(3)
    for c in ay2:
        c.wait_recv()
    a_sib(2)
    go_group(2)
    gx = rcopy(gsend.at[1 - xl], grecv, GX, pair)
    gx.start()

    for c in atc:
        c.wait_recv()
    for c in ac:
        c.wait_recv()

    def w_block(b):
        out = None
        for s in range(2):
            for t in range(2):
                a = jnp.concatenate([atg[s, t, 0], atg[s, t, 1]], axis=0)
                d = dot_nn(a, ogg[s, b, t])
                out = d if out is None else out + d
        return out

    cp, cm = [], []

    def c_up(s):
        val = w_block((z + 4 - s) % NZ)
        if s > 0:
            cp[s - 1].wait_recv()
            val += crp[s - 1].astype(F32)
        cps[s] = val.astype(BF16)
        c = rcopy(cps.at[s], crp.at[s], CP + s, zp)
        c.start()
        cp.append(c)

    def c_down(s):
        val = w_block((z + 5 + s) % NZ)
        if s > 0:
            cm[s - 1].wait_recv()
            val += crm[s - 1].astype(F32)
        cms[s] = val.astype(BF16)
        c = rcopy(cms.at[s], crm.at[s], CM + s, zm)
        c.start()
        cm.append(c)

    c_up(0)
    c_down(0)

    gx.wait_recv()

    def g_phase(i, _):
        cols = head_cols(i)
        go = gacc[xl, :, cols] + grecv[:, cols].astype(F32)
        r = rd[i]
        gb = (go * r).astype(BF16)
        gnb[i] = gb
        g = -jnp.sum(go * attn[i], axis=-1, keepdims=True) * r
        gd[i] = g
        qb = qf[i]
        put_state(st2, i, dot_tn(qb, gb), jnp.sum(qb.astype(F32) * g, axis=0, keepdims=True))
        return 0

    lax.fori_loop(0, HL, g_phase, 0)
    scan_send(st2, rv2, D2A)

    c_up(1)
    c_down(1)

    def back(i, x_ref, w, out_ref):
        hi = w.astype(BF16)
        lo = (w - hi.astype(F32)).astype(BF16)
        t = dot_nn(hi, wc[i]) + dot_nn(lo, wc[i])
        u = t[:, 0:DH] + t[:, DH:2 * DH]
        xf = x_ref[:, head_cols(i)].astype(F32) * C
        out_ref[:, head_cols(i)] = (C * (u - xf * jnp.sum(w, axis=-1, keepdims=True))).astype(BF16)

    def dq_phase(i, _):
        gb, g, kb, qb = gnb[i], gd[i], kf[i], qf[i]
        s, zrow = get_state(pr, i)
        bm = jnp.where(tri, dot_nt(gb, v_ref[:, head_cols(i)]) + g, 0.0).astype(BF16)
        dq = dot_nn(bm, kb) + dot_nt(gb, s) + g * zrow
        back(i, q_ref, dq * pq[i], qg_ref)
        dk0[i] = dot_tn(bm, qb)
        dv0[i] = dot_tn(ab[i], gb)
        return 0

    lax.fori_loop(0, 2, dq_phase, 0)

    scan_recv(st2, rv2, D2A)
    rv2[ctx] = st2[ctx]
    running(rv2, po2, True)
    pr2[ctx] = po2[ctx]
    scan_send(po2, pr2, D2B)

    c_up(2)
    c_down(2)
    lax.fori_loop(2, HL, dq_phase, 0)
    c_up(3)

    scan_recv(po2, pr2, D2B)

    def dk_phase(i, _):
        s, zrow = get_state(pr2, i)
        vb = v_ref[:, head_cols(i)]
        dk = dk0[i] + dot_nt(vb, s) + zrow
        back(i, k_ref, dk * pk[i], kg_ref)
        vg_ref[:, head_cols(i)] = (dv0[i] + dot_nn(kf[i], s)).astype(BF16)
        return 0

    lax.fori_loop(0, HL, dk_phase, 0)

    own = w_block(z)
    cp[3].wait_recv()
    cm[2].wait_recv()
    wg_ref[rows_r, :] = (own + crp[3].astype(F32) + crm[2].astype(F32)).astype(BF16)
    cc = rcopy(wg_ref.at[rows_r], wg_ref.at[rows_r], CC, sib)
    cc.start()

    for c in ax + bzp + bzm + list(ayp.values()) + list(aym.values()) + ay2 + bc + ac + atc + [gx] + cp + cm:
        c.wait_send()
    scan_sent(st, rv, D1A)
    scan_sent(po, pr, D1B)
    scan_sent(st2, rv2, D2A)
    scan_sent(po2, pr2, D2B)
    cc.wait()


def on_device(queries, key_vecs, values, out_grad, out_weight, sign_bits):
    flat = lambda a: a.reshape(T, HL * DH)
    vm = pl.BlockSpec(memory_space=pltpu.VMEM)
    state = pltpu.VMEM((NC, SL, DH), BF16)
    heads = lambda n, dt: pltpu.VMEM((HL, T, n), dt)
    blocks = lambda n: pltpu.VMEM((n, T, 256), BF16)
    qg, kg, vg, wg = pl.pallas_call(
        kernel,
        out_shape=[jax.ShapeDtypeStruct((T, HL * DH), BF16)] * 3
        + [jax.ShapeDtypeStruct((HL * DH, 256), BF16)],
        in_specs=[vm] * 6,
        out_specs=[vm] * 4,
        scratch_shapes=[
            pltpu.VMEM((2, 8, 2, T, 256), BF16),
            pltpu.VMEM((NZ, 512, 256), BF16),
            pltpu.VMEM((2, T, 512), F32),
            pltpu.VMEM((2, T, 512), BF16),
            pltpu.VMEM((T, 512), BF16),
            state, state, state, state, state, state, state, state,
            heads(256, BF16),
            heads(M, F32), heads(M, F32), heads(M, BF16), heads(M, BF16),
            heads(T, BF16), heads(DH, F32), heads(1, F32), heads(1, F32),
            heads(DH, F32),
            pltpu.VMEM((HL, DH, T), BF16),
            pltpu.VMEM((2, 2, 2, DH, T), BF16),
            heads(DH, BF16), heads(1, F32), heads(M, F32), heads(DH, F32),
            blocks(4), blocks(3), blocks(4), blocks(3),
            pltpu.SemaphoreType.DMA((NSEM,)),
            pltpu.SemaphoreType.DMA((NSEM,)),
        ],
        compiler_params=pltpu.CompilerParams(
            collective_id=0, has_side_effects=True, vmem_limit_bytes=48 * 1024 * 1024),
        cost_estimate=pl.CostEstimate(
            flops=5 * 10**9, bytes_accessed=4 * 10**6, transcendentals=5 * 10**5),
        name="performer_back",
    )(flat(queries), flat(key_vecs), flat(values), flat(out_grad), out_weight, sign_bits)
    shaped = lambda a: a.reshape(1, T, HL * DH)
    return shaped(qg), shaped(kg), shaped(vg), wg


def solution(mesh):
    tok = P("rep", "ctx", "head")
    return jax.shard_map(
        on_device, mesh=mesh,
        in_specs=(tok, tok, tok, tok, P("head", "ctx"), P("head", None, None)),
        out_specs=(tok, tok, tok, P("head", "ctx")),
        check_vma=False,
    )
```

time: 787 us -> 89.7 us (0.11)
  waiting for transfers between devices: 614 us -> 0 us
  Pallas kernels: 0 us -> 80.5 us
  blocking collectives: 67.6 us -> 0 us
  other arithmetic: 39.4 us -> 0 us
  matrix products: 33.3 us -> 0 us
  between operations: 14.2 us -> 0.65 us
    all_gather x4 -> x0, waiting for transfers between devices: 458 us -> none  [the longest x2 324 us: prefix(): pieces = jax.tree.map(lambda part: lax.all_gather(part, axis), value)]
    reduce_scatter x1 -> x0, waiting for transfers between devices: 154 us -> none  [on_device(): lax.psum_scatter(bmix('tc,tr->cr', cols, attn_flat), 'ctx', scatter_dimen...]
    pallas_call x0 -> x1, Pallas kernels: none -> 80.5 us  [on_device(): pl.pallas_call(kernel, out_shape=[jax.ShapeDtypeStruct((T, HL * DH), BF16...]
    all_gather x2 -> x0, blocking collectives: 61 us -> none  [prefix(): pieces = jax.tree.map(lambda part: lax.all_gather(part, axis), value)]
    select_n x60 -> x0, other arithmetic: 37.2 us -> none  [step(): jnp.where(position < mine, new, old)]
    dot_general x23 -> x0, matrix products: 28.4 us -> none  [the longest x13 18.5 us: bmix(): return jnp.einsum(form, left, right, preferred_element_type=jnp.float32)]
  transfers between devices with their start and end apart: 5 -> 0, of which waited for: 5 -> 0; matrix products, arithmetic and copies ran while one was open for 8% -> 0% of each run, Pallas kernels for 0% -> 0%
where the time goes in v1:
time: 89.7 us; the launch traced here: 89.4 us
  Pallas kernels  80.5 us (90%)
  local copies, waits for them, and re-layouts  8.27 us (9%)
    pallas_call x1, Pallas kernels, on_device(): pl.pallas_call(kernel, out_shape=[jax.ShapeDtypeStruct((T, HL * DH), BF16...  80.5 us
    unnamed x15, local copies, waits for them, and re-layouts  8.27 us

profile of v1, /device:TPU:1, one launch (start us, length us, event | category | flops | bytes accessed | tf_op | source)
XLA Modules:
  0.0 89.4 jit_solution(3593055925000800535)
XLA Ops:
  0.6 0.7 copy.10.sb_ref
  1.3 0.0 copy-start
  1.3 0.9 %copy-done = bf16[1,256,512]{2,1,0:T(8,128)(2,1)S(1)} copy-done((bf16[1,256,512]{2,1,0:T(8,128)(2,1)S(1)}, bf16[1,256,512]{2,1,0:T(8,128)(2,1)}, u32[]{:S(2)}) %copy-start) | copy-done | bytes 262168
  2.3 0.0 copy-start.1
  2.3 0.9 %copy-done.1 = bf16[1,256,512]{2,1,0:T(8,128)(2,1)S(1)} copy-done((bf16[1,256,512]{2,1,0:T(8,128)(2,1)S(1)}, bf16[1,256,512]{2,1,0:T(8,128)(2,1)}, u32[]{:S(2)}) %copy-start.1) | copy-done | bytes 262168
  3.2 0.0 copy-start.2
  3.2 0.9 %copy-done.2 = bf16[1,256,512]{2,1,0:T(8,128)(2,1)S(1)} copy-done((bf16[1,256,512]{2,1,0:T(8,128)(2,1)S(1)}, bf16[1,256,512]{2,1,0:T(8,128)(2,1)}, u32[]{:S(2)}) %copy-start.2) | copy-done | bytes 262168
  4.2 0.0 copy-start.3
  4.2 0.9 %copy-done.3 = bf16[1,256,512]{2,1,0:T(8,128)(2,1)S(1)} copy-done((bf16[1,256,512]{2,1,0:T(8,128)(2,1)S(1)}, bf16[1,256,512]{2,1,0:T(8,128)(2,1)}, u32[]{:S(2)}) %copy-start.3) | copy-done | bytes 262168
  5.1 0.0 copy-start.4
  5.1 0.9 %copy-done.4 = bf16[512,256]{1,0:T(8,128)(2,1)S(1)} copy-done((bf16[512,256]{1,0:T(8,128)(2,1)S(1)}, bf16[512,256]{1,0:T(8,128)(2,1)}, u32[]{:S(2)}) %copy-start.4) | copy-done | bytes 262168
  6.1 80.5 %performer_back.1 = (bf16[256,512]{1,0:T(8,128)(2,1)S(1)}, bf16[256,512]{1,0:T(8,128)(2,1)S(1)}, bf16[256,512]{1,0:T(8,128)(2,1)S(1)}, bf16[512,256]{1,0:T(8,128)(2,1)S(1)}) custom-call(bf16[256,512]{1,0:T(8,128)(2,1)S(1)} %bitcast.10, bf16[256,512]{1,0:T(8,128)(2,1)S(1)} %bitcast.11, bf16[256,512]{1,0:T(8,128)(2,1)S(1)} %bitcast.12, ...), custom_call_target="tpu_custom_call" | custom-call | flops 5000000000 | bytes 4000000 | tf_op jit(solution)/shard_map/performer_back/pallas_call | solution.py:492
  86.6 0.7 copy.15
  87.3 0.7 copy.16
  88.0 0.7 copy.17
  88.7 0.7 copy.18
Async XLA Ops:
  1.3 0.9 %copy-start = (bf16[1,256,512]{2,1,0:T(8,128)(2,1)S(1)}, bf16[1,256,512]{2,1,0:T(8,128)(2,1)}, u32[]{:S(2)}) copy-start(bf16[1,256,512]{2,1,0:T(8,128)(2,1)} %param.6) | copy-start | bytes 786436
  2.3 0.9 %copy-start.1 = (bf16[1,256,512]{2,1,0:T(8,128)(2,1)S(1)}, bf16[1,256,512]{2,1,0:T(8,128)(2,1)}, u32[]{:S(2)}) copy-start(bf16[1,256,512]{2,1,0:T(8,128)(2,1)} %param.7) | copy-start | bytes 786436
  3.2 0.9 %copy-start.2 = (bf16[1,256,512]{2,1,0:T(8,128)(2,1)S(1)}, bf16[1,256,512]{2,1,0:T(8,128)(2,1)}, u32[]{:S(2)}) copy-start(bf16[1,256,512]{2,1,0:T(8,128)(2,1)} %param.8) | copy-start | bytes 786436
  4.2 0.9 %copy-start.3 = (bf16[1,256,512]{2,1,0:T(8,128)(2,1)S(1)}, bf16[1,256,512]{2,1,0:T(8,128)(2,1)}, u32[]{:S(2)}) copy-start(bf16[1,256,512]{2,1,0:T(8,128)(2,1)} %param.9) | copy-start | bytes 786436
  5.1 0.9 %copy-start.4 = (bf16[512,256]{1,0:T(8,128)(2,1)S(1)}, bf16[512,256]{1,0:T(8,128)(2,1)}, u32[]{:S(2)}) copy-start(bf16[512,256]{1,0:T(8,128)(2,1)} %ow_ref.1) | copy-start | bytes 786436

commit v2 on v1

v2 whole, which is shorter than its diff:
```python
import functools

import jax
import jax.numpy as jnp
from jax import lax
from jax.experimental import pallas as pl
from jax.experimental.pallas import tpu as pltpu
from jax.sharding import PartitionSpec as P

DH = 128
M = 256
T = 256
HL = 4
NZ = 8
NC = 16
SR = 32
C = DH ** (-0.25)
F32 = jnp.float32
BF16 = jnp.bfloat16
MESH = pl.DeviceIdType.MESH

AX = 0
AYP, AYM, AYP2, AYM2 = 4, 8, 12, 14
AC = 16
BZP, BZM, BC = 20, 24, 27
GX, ATS, ATP = 34, 35, 36
CP, CM, CC = 38, 46, 52
D1A, D1B, D2A, D2B = 54, 56, 58, 60
ZB, RB = 62, 78
NSEM = 94


def dot_nn(a, b):
    return lax.dot_general(a, b, (((1,), (0,)), ((), ())), preferred_element_type=F32)


def dot_nt(a, b):
    return lax.dot_general(a, b, (((1,), (1,)), ((), ())), preferred_element_type=F32)


def dot_tn(a, b):
    return lax.dot_general(a, b, (((0,), (0,)), ((), ())), preferred_element_type=F32)


def hadamard():
    i = lax.broadcasted_iota(jnp.int32, (DH, DH), 0)
    j = lax.broadcasted_iota(jnp.int32, (DH, DH), 1)
    x = i & j
    x = x ^ (x >> 4)
    x = x ^ (x >> 2)
    x = x ^ (x >> 1)
    return (1 - 2 * (x & 1)).astype(F32)


def head_cols(i):
    return pl.ds(pl.multiple_of(i * DH, DH), DH)


def kernel(q_hbm, k_hbm, v_hbm, og_hbm, ow_hbm, sb_hbm,
           qg_ref, kg_ref, vg_ref, wg_ref,
           q_ref, k_ref, v_ref, sb_ref,
           ogg, owg, gacc, gsend, grecv,
           st, rv, po, pr, st2, rv2, po2, pr2, zs, zr, rs2, rr2, zpre,
           wc, pq, pk, qf, kf, ab, nv, rs, rd, attn, at, atg,
           gnb, gd, dk0, dv0, cps, cms, crp, crm,
           ssem, rsem, lsem):
    ctx = lax.axis_index("ctx")
    head = lax.axis_index("head")
    rep = lax.axis_index("rep")
    z, xl = ctx // 2, ctx % 2
    y, xh = head // 2, head % 2
    x = xh * 2 + xl
    sib = {"rep": 1 - rep}
    pair_ctx = z * 2 + 1 - xl
    pair = {"ctx": pair_ctx}
    pair_sib = {"ctx": pair_ctx, "rep": 1 - rep}
    yp = {"head": (head + 2) % 8}
    ym = {"head": (head + 6) % 8}
    zp = {"ctx": (ctx + 2) % NC}
    zm = {"ctx": (ctx + NC - 2) % NC}

    def xdev(k):
        xx = (x + k) % 4
        return {"ctx": z * 2 + xx % 2, "head": y * 2 + xx // 2}

    def rcopy(src, dst, n, dev):
        return pltpu.make_async_remote_copy(
            src_ref=src, dst_ref=dst, send_sem=ssem.at[n], recv_sem=rsem.at[n],
            device_id=dev, device_id_type=MESH)

    barrier = pltpu.get_barrier_semaphore()

    def greet(d, _):
        pl.semaphore_signal(barrier, inc=1, device_id={"ctx": (ctx + d) % NC}, device_id_type=MESH)
        return 0

    lax.fori_loop(1, NC, greet, 0)
    for dev in (sib, pair_sib, yp, ym):
        pl.semaphore_signal(barrier, inc=1, device_id=dev, device_id_type=MESH)
    for k in range(1, 4):
        xx = (x + k) % 4

        @pl.when(xx // 2 != xh)
        def _():
            pl.semaphore_signal(barrier, inc=1, device_id=xdev(k), device_id_type=MESH)

    def half(s):
        return og_hbm.at[:, pl.ds(pl.multiple_of(s * 256, 256), 256)]

    my_b = head
    rows_r = pl.ds(pl.multiple_of(rep * 256, 256), 256)
    local = [pltpu.make_async_copy(a, b, lsem.at[n]) for n, (a, b) in enumerate((
        (sb_hbm, sb_ref), (k_hbm, k_ref), (v_hbm, v_ref), (q_hbm, q_ref),
        (half(xl), ogg.at[0, my_b, xl]), (ow_hbm, owg.at[z])))]
    for c in local:
        c.start()

    hd = hadamard()
    hb = hd.astype(BF16)

    def mixing(i, _):
        bits = sb_ref[i].astype(F32) * 2.0 - 1.0
        for blk in range(2):
            s = bits[:, blk * DH:(blk + 1) * DH]
            inner = dot_nn((hd * s[1:2]).astype(BF16), hb).astype(BF16)
            w = dot_nn((hd * s[0:1]).astype(BF16), inner) * (s[2:3] * (1.0 / DH))
            hi = w.astype(BF16)
            lo = (w - hi.astype(F32)).astype(BF16)
            wc[i, blk * DH:(blk + 1) * DH, 0:DH] = hi
            wc[i, blk * DH:(blk + 1) * DH, DH:2 * DH] = lo
        return 0

    local[0].wait()
    lax.fori_loop(0, HL, mixing, 0)

    def features(x_ref, i):
        xb = x_ref[:, head_cols(i)]
        xf = xb.astype(F32)
        proj = dot_nt(jnp.concatenate([xb, xb], axis=1), wc[i]) * C
        norm = jnp.sum(xf * xf, axis=-1, keepdims=True) * (0.5 * C * C)
        return jnp.exp(proj - norm) * (1.0 / 16.0)

    def put_state(buf, i, s):
        sb = s.astype(BF16)
        for t in range(8):
            buf[i // 2, i % 2 * 8 + t] = sb[SR * t:SR * (t + 1)]

    def get_state(buf, i):
        return jnp.concatenate(
            [buf[i // 2, (ctx + NC - (i % 2 * 8 + t)) % NC] for t in range(8)], axis=0)

    def put_row(buf, i, row):
        buf[2 * i:2 * i + 1, :] = row[:, 0:DH]
        buf[2 * i + 1:2 * i + 2, :] = row[:, DH:2 * DH]

    def get_row(value, i):
        return jnp.concatenate([value[2 * i:2 * i + 1], value[2 * i + 1:2 * i + 2]], axis=1)

    local[1].wait()
    local[2].wait()
    for i in range(HL):
        p = features(k_ref, i)
        pk[i] = p
        kb = p.astype(BF16)
        kf[i] = kb
        put_state(st, i, dot_tn(kb, v_ref[:, head_cols(i)]))
        put_row(zs, i, jnp.sum(kb.astype(F32), axis=0, keepdims=True))

    def scan_send(src, dst, n, h):
        def go(d, _):
            to = (ctx + d) % NC
            rcopy(src.at[h, to], dst.at[h, d], n + h, {"ctx": to}).start()
            return 0

        lax.fori_loop(1, NC, go, 0)

    def scan_all(src, dst, n, h):
        rest = pl.ds(1, NC - 1)
        return rcopy(src.at[h, rest], dst.at[h, rest], n + h, pair)

    def running(rbuf, obuf, h, backward):
        def step(n, cs):
            c = NC - 1 - n if backward else n
            obuf[h, c] = cs.astype(BF16)
            return cs + rbuf[h, (ctx + NC - c) % NC].astype(F32)

        lax.fori_loop(0, NC, step, jnp.zeros((SR, DH), F32))

    def row_copy(src, dst, n, d, sign):
        return rcopy(src, dst.at[d], n + d, {"ctx": (ctx + sign * d + NC) % NC})

    def each(count, fn):
        lax.fori_loop(1, count + 1, lambda d, _: (fn(d), 0)[1], 0)

    pl.semaphore_wait(barrier, 21)

    later, earlier = NC - 1 - ctx, ctx
    each(later, lambda d: row_copy(zs, zr, ZB, d, 1).start())
    scan_send(st, rv, D1A, 0)

    ax = {}
    for k in (1, 3, 2):
        xx = (x + k) % 4
        ax[k] = rcopy(half(xx % 2), ogg.at[0, my_b, xl], AX + k, xdev(k))
        ax[k].start()

    def piece(yy, k):
        xx = (x + 4 - k) % 4
        return ogg.at[0, yy * 2 + xx // 2, xx % 2]

    ayp, aym, ay2 = {}, {}, {}

    def y_send(k):
        p = piece(y, k)
        src = half(xl) if k == 0 else p
        ayp[k] = rcopy(src, p, AYP + k, yp)
        aym[k] = rcopy(src, p, AYM + k, ym)
        ayp[k].start()
        aym[k].start()

    def y_relay(k):
        up = k < 2
        (ayp if up else aym)[k].wait_recv()
        p = piece((y + 3) % 4 if up else (y + 1) % 4, k)
        ay2[k] = rcopy(p, p, AYP2 + k if up else AYM2 + k - 2, yp if up else ym)
        ay2[k].start()

    y_send(0)

    bzp, bzm, bc = [], [], []

    def z_send(s, up):
        blk = (z + NZ - s) % NZ if up else (z + s) % NZ
        ref = owg.at[blk, rows_r]
        c = rcopy(ow_hbm.at[rows_r] if s == 0 else ref, ref,
                  (BZP if up else BZM) + s, zp if up else zm)
        c.start()
        (bzp if up else bzm).append(c)

    def b_recv(s, up):
        (bzp if up else bzm)[s].wait_recv()
        blk = (z + NZ - 1 - s) % NZ if up else (z + 1 + s) % NZ
        ref = owg.at[blk, rows_r]
        if s + 1 < (4 if up else 3):
            z_send(s + 1, up)
        c = rcopy(ref, ref, BC + (s if up else 4 + s), sib)
        c.start()
        bc.append(c)

    z_send(0, True)
    z_send(0, False)
    scan_send(st, rv, D1A, 1)

    tri = (lax.broadcasted_iota(jnp.int32, (T, T), 0)
           >= lax.broadcasted_iota(jnp.int32, (T, T), 1))

    def q_phase(i, _):
        p = features(q_ref, i)
        pq[i] = p
        qb = p.astype(BF16)
        qf[i] = qb
        am = jnp.where(tri, dot_nt(qb, kf[i]), 0.0)
        rs[i] = jnp.sum(am, axis=-1, keepdims=True)
        amb = am.astype(BF16)
        ab[i] = amb
        nv[i] = dot_nn(amb, v_ref[:, head_cols(i)])
        return 0

    local[3].wait()
    lax.fori_loop(0, 2, q_phase, 0)

    for k in (1, 3, 2):
        ax[k].wait_recv()
        y_send(k)
    b_recv(0, True)
    b_recv(0, False)

    lax.fori_loop(2, HL, q_phase, 0)

    each(earlier, lambda d: row_copy(zs, zr, ZB, d, 1).wait_recv())
    zsum = lax.fori_loop(1, ctx + 1, lambda d, a: a + zr[d], jnp.zeros((8, DH), F32))
    zpre[...] = zsum
    for i in range(HL):
        den = rs[i] + jnp.sum(qf[i].astype(F32) * get_row(zsum, i), axis=-1, keepdims=True)
        rd[i] = 1.0 / den

    def scan_turn(src, rbuf, obuf, dst, na, nb, h, backward):
        scan_all(src, rbuf, na, h).wait_recv()
        rbuf[h, 0] = src[h, ctx]
        running(rbuf, obuf, h, backward)
        dst[h, 0] = obuf[h, ctx]
        scan_send(obuf, dst, nb, h)

    ac = []

    def a_sib(n):
        yy = (y + n) % 4
        c = rcopy(ogg.at[0, pl.ds(yy * 2, 2)], ogg.at[1, pl.ds(yy * 2, 2)], AC + n, sib)
        c.start()
        ac.append(c)

    y_relay(1)
    y_relay(3)
    scan_turn(st, rv, po, pr, D1A, D1B, 0, False)
    b_recv(1, True)
    b_recv(1, False)
    y_relay(0)
    y_relay(2)
    scan_turn(st, rv, po, pr, D1A, D1B, 1, False)
    local[4].wait()
    local[5].wait()
    a_sib(0)
    b_recv(2, True)
    b_recv(2, False)
    b_recv(3, True)

    def go_part(mine):
        tok = xl if mine else 1 - xl

        def tile(m, _):
            rows = pl.ds(pl.multiple_of(m * 128, 128), 128)
            acc = dot_nt(ogg[0, 0, tok, rows, :], owg[0])
            for b in range(1, 8):
                acc += dot_nt(ogg[0, b, tok, rows, :], owg[b])
            if mine:
                gacc[rows, :] = acc
            else:
                gsend[rows, :] = acc.astype(BF16)
            return 0

        lax.fori_loop(0, 2, tile, 0)

    for c in bc:
        c.wait_recv()
    for k in (1, 3):
        (aym if k < 2 else ayp)[k].wait_recv()
        ay2[k].wait_recv()
    go_part(False)
    gx = rcopy(gsend, grecv, GX, pair)
    gx.start()

    atp = []
    ats = rcopy(at.at[pl.ds((1 - rep) * 2, 2)], atg.at[1, xl], ATS, sib)

    def attn_chunk(h):
        scan_all(po, pr, D1B, h).wait_recv()
        for i in (2 * h, 2 * h + 1):
            a = (nv[i] + dot_nn(qf[i], get_state(pr, i))) * rd[i]
            attn[i] = a
            at[i] = a.astype(BF16).T
        src = at.at[pl.ds(h * 2, 2)]
        c = rcopy(src, atg.at[(rep + h) % 2, xl], ATP + (rep + h) % 2, {"ctx": pair_ctx, "rep": h})
        c.start()
        atp.append(c)

        @pl.when(rep != h)
        def _():
            ats.start()

        @pl.when(rep == h)
        def _():
            atg[0, xl] = at[h * 2:h * 2 + 2]

    attn_chunk(0)
    attn_chunk(1)

    for k in (0, 2):
        (aym if k < 2 else ayp)[k].wait_recv()
        ay2[k].wait_recv()
    a_sib(1)
    a_sib(3)
    a_sib(2)
    go_part(True)

    gx.wait_recv()

    def g_chunk(h):
        for i in (2 * h, 2 * h + 1):
            cols = head_cols(i)
            go = gacc[:, cols] + grecv[:, cols].astype(F32)
            r = rd[i]
            gb = (go * r).astype(BF16)
            gnb[i] = gb
            g = -jnp.sum(go * attn[i], axis=-1, keepdims=True) * r
            gd[i] = g
            qb = qf[i]
            put_state(st2, i, dot_tn(qb, gb))
            put_row(rs2, i, jnp.sum(qb.astype(F32) * g, axis=0, keepdims=True))
        scan_send(st2, rv2, D2A, h)

    g_chunk(0)
    g_chunk(1)
    each(earlier, lambda d: row_copy(rs2, rr2, RB, d, -1).start())

    ats.wait_recv()
    for n in range(2):
        rcopy(atg.at[n, xl], atg.at[n, xl], ATP + n, pair).wait_recv()
    for c in ac:
        c.wait_recv()

    def w_block(b, ch):
        out = None
        for s in range(2):
            for t in range(2):
                d = dot_nn(atg[s, t, ch], ogg[s, b, t])
                out = d if out is None else out + d
        return out

    cp, cm = {}, {}

    def c_step(s, ch, up):
        sb, rb, cc = (cps, crp, cp) if up else (cms, crm, cm)
        val = w_block((z + 4 - s) % NZ if up else (z + 5 + s) % NZ, ch)
        if s > 0:
            cc[s - 1, ch].wait_recv()
            val += rb[s - 1, ch].astype(F32)
        sb[s, ch] = val.astype(BF16)
        c = rcopy(sb.at[s, ch], rb.at[s, ch], (CP if up else CM) + 2 * s + ch, zp if up else zm)
        c.start()
        cc[s, ch] = c

    def c_round(s):
        for ch in range(2):
            c_step(s, ch, True)
            if s < 3:
                c_step(s, ch, False)

    c_round(0)

    def back(i, x_ref, w, out_ref):
        hi = w.astype(BF16)
        lo = (w - hi.astype(F32)).astype(BF16)
        t = dot_nn(hi, wc[i]) + dot_nn(lo, wc[i])
        u = t[:, 0:DH] + t[:, DH:2 * DH]
        xf = x_ref[:, head_cols(i)].astype(F32) * C
        out_ref[:, head_cols(i)] = (C * (u - xf * jnp.sum(w, axis=-1, keepdims=True))).astype(BF16)

    def dq_phase(i):
        gb, g, kb, qb = gnb[i], gd[i], kf[i], qf[i]
        bm = jnp.where(tri, dot_nt(gb, v_ref[:, head_cols(i)]) + g, 0.0).astype(BF16)
        dq = dot_nn(bm, kb) + dot_nt(gb, get_state(pr, i)) + g * get_row(zpre[...], i)
        back(i, q_ref, dq * pq[i], qg_ref)
        dk0[i] = dot_tn(bm, qb)
        dv0[i] = dot_tn(ab[i], gb)

    dq_phase(0)
    c_round(1)
    dq_phase(1)

    scan_turn(st2, rv2, po2, pr2, D2A, D2B, 0, True)
    c_round(2)
    scan_turn(st2, rv2, po2, pr2, D2A, D2B, 1, True)
    dq_phase(2)
    c_round(3)
    dq_phase(3)

    each(later, lambda d: row_copy(rs2, rr2, RB, d, -1).wait_recv())
    rsum = lax.fori_loop(1, later + 1, lambda d, a: a + rr2[d], jnp.zeros((8, DH), F32))

    ccs = []

    def c_last(ch):
        own = w_block(z, ch)
        cp[3, ch].wait_recv()
        cm[2, ch].wait_recv()
        rows = pl.ds(pl.multiple_of(rep * 256 + ch * DH, DH), DH)
        wg_ref[rows, :] = (own + crp[3, ch].astype(F32) + crm[2, ch].astype(F32)).astype(BF16)
        c = rcopy(wg_ref.at[rows], wg_ref.at[rows], CC + ch, sib)
        c.start()
        ccs.append(c)

    def dk_chunk(h):
        scan_all(po2, pr2, D2B, h).wait_recv()
        for i in (2 * h, 2 * h + 1):
            s = get_state(pr2, i)
            vb = v_ref[:, head_cols(i)]
            dk = dk0[i] + dot_nt(vb, s) + get_row(rsum, i)
            back(i, k_ref, dk * pk[i], kg_ref)
            vg_ref[:, head_cols(i)] = (dv0[i] + dot_nn(kf[i], s)).astype(BF16)

    dk_chunk(0)
    c_last(0)
    c_last(1)
    dk_chunk(1)

    for group in (ax, ayp, aym, ay2, cp, cm):
        for c in group.values():
            c.wait_send()
    for c in bzp + bzm + bc + ac + atp + [ats, gx]:
        c.wait_send()
    for h in range(2):
        for src, dst, n in ((st, rv, D1A), (po, pr, D1B), (st2, rv2, D2A), (po2, pr2, D2B)):
            scan_all(src, dst, n, h).wait_send()
    each(later, lambda d: row_copy(zs, zr, ZB, d, 1).wait_send())
    each(earlier, lambda d: row_copy(rs2, rr2, RB, d, -1).wait_send())
    for c in ccs:
        c.wait()


def store(*refs):
    n = (len(refs) - 1) // 2
    copies = [pltpu.make_async_copy(refs[i], refs[n + i], refs[-1].at[i]) for i in range(n)]
    for c in copies:
        c.start()
    for c in copies:
        c.wait()


def on_device(queries, key_vecs, values, out_grad, out_weight, sign_bits):
    flat = lambda a: a.reshape(T, HL * DH)
    hbm = pl.BlockSpec(memory_space=pltpu.HBM)
    vm = pl.BlockSpec(memory_space=pltpu.VMEM)
    state = pltpu.VMEM((2, NC, SR, DH), BF16)
    row = pltpu.VMEM((8, DH), F32)
    rows = pltpu.VMEM((NC, 8, DH), F32)
    heads = lambda n, dt: pltpu.VMEM((HL, T, n), dt)
    blocks = lambda n: pltpu.VMEM((n, 2, DH, 256), BF16)
    act = pltpu.VMEM((T, HL * DH), BF16)
    shapes = [jax.ShapeDtypeStruct((T, HL * DH), BF16)] * 3 + [jax.ShapeDtypeStruct((HL * DH, 256), BF16)]
    grads = pl.pallas_call(
        kernel,
        out_shape=shapes,
        in_specs=[hbm] * 6,
        out_specs=[vm] * 4,
        scratch_shapes=[
            act, act, act, pltpu.VMEM((HL, 3, M), jnp.int32),
            pltpu.VMEM((2, 8, 2, T, 256), BF16),
            pltpu.VMEM((NZ, 512, 256), BF16),
            pltpu.VMEM((T, 512), F32),
            act, act,
            state, state, state, state, state, state, state, state,
            row, rows, row, rows, row,
            heads(256, BF16),
            heads(M, F32), heads(M, F32), heads(M, BF16), heads(M, BF16),
            heads(T, BF16), heads(DH, F32), heads(1, F32), heads(1, F32),
            heads(DH, F32),
            pltpu.VMEM((HL, DH, T), BF16),
            pltpu.VMEM((2, 2, 2, DH, T), BF16),
            heads(DH, BF16), heads(1, F32), heads(M, F32), heads(DH, F32),
            blocks(4), blocks(3), blocks(4), blocks(3),
            pltpu.SemaphoreType.DMA((NSEM,)),
            pltpu.SemaphoreType.DMA((NSEM,)),
            pltpu.SemaphoreType.DMA((6,)),
        ],
        compiler_params=pltpu.CompilerParams(
            collective_id=0, has_side_effects=True, vmem_limit_bytes=62 * 1024 * 1024),
        cost_estimate=pl.CostEstimate(
            flops=5 * 10**9, bytes_accessed=4 * 10**6, transcendentals=5 * 10**5),
        name="performer_back",
    )(flat(queries), flat(key_vecs), flat(values), flat(out_grad), out_weight, sign_bits)
    qg, kg, vg, wg = pl.pallas_call(
        store,
        out_shape=shapes,
        in_specs=[vm] * 4,
        out_specs=[hbm] * 4,
        scratch_shapes=[pltpu.SemaphoreType.DMA((4,))],
        name="store",
    )(*grads)
    shaped = lambda a: a.reshape(1, T, HL * DH)
    return shaped(qg), shaped(kg), shaped(vg), wg


def solution(mesh):
    tok = P("rep", "ctx", "head")
    return jax.shard_map(
        on_device, mesh=mesh,
        in_specs=(tok, tok, tok, tok, P("head", "ctx"), P("head", None, None)),
        out_specs=(tok, tok, tok, P("head", "ctx")),
        check_vma=False,
    )
```

time: 89.7 us -> 80.8 us (0.901)
  local copies, waits for them, and re-layouts: 8.27 us -> 1.32 us
  Pallas kernels: 80.5 us -> 78.5 us
    unnamed x15 -> x1, local copies, waits for them, and re-layouts: 8.27 us -> 1.32 us
    pallas_call x1 -> x2, Pallas kernels: 80.5 us -> 78.5 us  [the longest x1 76.4 us: on_device(): pl.pallas_call(kernel, out_shape=shapes, in_specs=[hbm] * 6, out_specs=[v...]
where the time goes in v2:
time: 80.8 us; the launch traced here: 80.5 us
  Pallas kernels  78.5 us (97%)
  local copies, waits for them, and re-layouts  1.32 us (2%)
    pallas_call x1, Pallas kernels, on_device(): pl.pallas_call(kernel, out_shape=shapes, in_specs=[hbm] * 6, out_specs=[v...  76.4 us
    pallas_call x1, Pallas kernels, on_device(): pl.pallas_call(store, out_shape=shapes, in_specs=[vm] * 4, out_specs=[hbm...  2.18 us

profile of v2, /device:TPU:1, one launch (start us, length us, event | category | flops | bytes accessed | tf_op | source)
XLA Modules:
  0.0 80.5 jit_solution(14725361135891746402)
XLA Ops:
  0.6 1.3 %copy.10.sb_hbm = s32[4,3,256]{2,1,0:T(4,128)} copy(s32[4,3,256]{2,0,1:T(4,128)} %param.11) | data formatting | bytes 24576 | tf_op args[5]
  1.9 76.4 %performer_back.1 = (bf16[256,512]{1,0:T(8,128)(2,1)}, bf16[256,512]{1,0:T(8,128)(2,1)}, bf16[256,512]{1,0:T(8,128)(2,1)}, bf16[512,256]{1,0:T(8,128)(2,1)}) custom-call(bf16[256,512]{1,0:T(8,128)(2,1)} %bitcast.7, bf16[256,512]{1,0:T(8,128)(2,1)} %bitcast.8, bf16[256,512]{1,0:T(8,128)(2,1)} %bitcast.9, bf16[256,512]{1,0:T(8,128)(2,1)} %bitcast.10, ...), custom_call_target="tpu_custom_call" | custom-call | flops 5000000000 | bytes 4000000 | tf_op jit(solution)/shard_map/performer_back/pallas_call | solution.py:520
  78.3 2.2 %store.1 = (bf16[256,512]{1,0:T(8,128)(2,1)}, bf16[256,512]{1,0:T(8,128)(2,1)}, bf16[256,512]{1,0:T(8,128)(2,1)}, bf16[512,256]{1,0:T(8,128)(2,1)}) custom-call(bf16[256,512]{1,0:T(8,128)(2,1)} %get-tuple-element.12.refs_0_, bf16[256,512]{1,0:T(8,128)(2,1)} %get-tuple-element.13.refs_1_, bf16[256,512]{1,0:T(8,128)(2,1)} %get-tuple-element.14.refs_2_, ...), custom_call_target="tpu_custom_call" | custom-call | tf_op jit(solution)/shard_map/store/pallas_call | solution.py:551

commit v3 on v2

v3 whole, which is shorter than its diff:
```python
import functools

import jax
import jax.numpy as jnp
from jax import lax
from jax.experimental import pallas as pl
from jax.experimental.pallas import tpu as pltpu
from jax.sharding import PartitionSpec as P

DH = 128
M = 256
T = 256
HL = 4
NZ = 8
NC = 16
C = DH ** (-0.25)
F32 = jnp.float32
BF16 = jnp.bfloat16
MESH = pl.DeviceIdType.MESH

AX, AYP, AYM, AY2, AC = 0, 4, 8, 12, 16
BZP, BZM, BC = 32, 36, 39
GX, ATS, ATP = 46, 47, 48
CP, CM, CC = 50, 58, 64
D1, D2 = 65, 74
ZB, RB = 83, 98
NSEM = 114


def dot_nn(a, b):
    return lax.dot_general(a, b, (((1,), (0,)), ((), ())), preferred_element_type=F32)


def dot_nt(a, b):
    return lax.dot_general(a, b, (((1,), (1,)), ((), ())), preferred_element_type=F32)


def dot_tn(a, b):
    return lax.dot_general(a, b, (((0,), (0,)), ((), ())), preferred_element_type=F32)


def hadamard():
    i = lax.broadcasted_iota(jnp.int32, (DH, DH), 0)
    j = lax.broadcasted_iota(jnp.int32, (DH, DH), 1)
    x = i & j
    x = x ^ (x >> 4)
    x = x ^ (x >> 2)
    x = x ^ (x >> 1)
    return (1 - 2 * (x & 1)).astype(F32)


def head_cols(i):
    return pl.ds(pl.multiple_of(i * DH, DH), DH)


def kernel(q_hbm, k_hbm, v_hbm, og_hbm, ow_hbm, sb_hbm,
           qg_hbm, kg_hbm, vg_hbm, wg_hbm,
           q_ref, k_ref, v_ref, sb_ref, qg_ref, kg_ref, vg_ref, wg_ref,
           ogg, owg, gacc, gsend, grecv,
           st, l1, l2, tot, pf, pr, st2, l12, l22, tot2, pf2, pr2, run, zs, zr, rs2, rr2, zpre,
           wc, pq, pk, qf, kf, ab, nv, rs, rd, attn, at, atg,
           gnb, gd, dk0, dv0, cps, cms, crp, crm,
           ssem, rsem, lsem):
    ctx = lax.axis_index("ctx")
    head = lax.axis_index("head")
    rep = lax.axis_index("rep")
    z, xl = ctx // 2, ctx % 2
    y, xh = head // 2, head % 2
    x = xh * 2 + xl
    sib = {"rep": 1 - rep}
    pair_ctx = z * 2 + 1 - xl
    pair = {"ctx": pair_ctx}
    pair_sib = {"ctx": pair_ctx, "rep": 1 - rep}
    yp = {"head": (head + 2) % 8}
    ym = {"head": (head + 6) % 8}
    zp = {"ctx": (ctx + 2) % NC}
    zm = {"ctx": (ctx + NC - 2) % NC}

    def xdev(k):
        xx = (x + k) % 4
        return {"ctx": z * 2 + xx % 2, "head": y * 2 + xx // 2}

    def rcopy(src, dst, n, dev):
        return pltpu.make_async_remote_copy(
            src_ref=src, dst_ref=dst, send_sem=ssem.at[n], recv_sem=rsem.at[n],
            device_id=dev, device_id_type=MESH)

    barrier = pltpu.get_barrier_semaphore()

    def greet(d, _):
        pl.semaphore_signal(barrier, inc=1, device_id={"ctx": (ctx + d) % NC}, device_id_type=MESH)
        return 0

    lax.fori_loop(1, NC, greet, 0)
    for dev in (sib, pair_sib, yp, ym):
        pl.semaphore_signal(barrier, inc=1, device_id=dev, device_id_type=MESH)
    for k in range(1, 4):
        xx = (x + k) % 4

        @pl.when(xx // 2 != xh)
        def _():
            pl.semaphore_signal(barrier, inc=1, device_id=xdev(k), device_id_type=MESH)

    def half(s):
        return og_hbm.at[:, pl.ds(pl.multiple_of(s * 256, 256), 256)]

    my_b = head
    rows_r = pl.ds(pl.multiple_of(rep * 256, 256), 256)
    local = [pltpu.make_async_copy(a, b, lsem.at[n]) for n, (a, b) in enumerate((
        (sb_hbm, sb_ref), (k_hbm, k_ref), (v_hbm, v_ref), (q_hbm, q_ref),
        (half(xl), ogg.at[0, my_b, xl]), (ow_hbm, owg.at[z])))]
    for c in local:
        c.start()

    hd = hadamard()
    hb = hd.astype(BF16)

    def mixing(i):
        for blk in range(2):
            s = [sb_ref[n, i:i + 1, blk * DH:(blk + 1) * DH].astype(F32) * 2.0 - 1.0 for n in range(3)]
            inner = dot_nn((hd * s[1]).astype(BF16), hb).astype(BF16)
            w = dot_nn((hd * s[0]).astype(BF16), inner) * (s[2] * (1.0 / DH))
            hi = w.astype(BF16)
            lo = (w - hi.astype(F32)).astype(BF16)
            wc[i, blk * DH:(blk + 1) * DH, 0:DH] = hi
            wc[i, blk * DH:(blk + 1) * DH, DH:2 * DH] = lo

    local[0].wait()
    for i in range(HL):
        mixing(i)

    def features(x_ref, i):
        xb = x_ref[:, head_cols(i)]
        xf = xb.astype(F32)
        proj = dot_nt(jnp.concatenate([xb, xb], axis=1), wc[i]) * C
        norm = jnp.sum(xf * xf, axis=-1, keepdims=True) * (0.5 * C * C)
        return jnp.exp(proj - norm) * (1.0 / 16.0)

    def put_row(buf, i, row):
        buf[2 * i:2 * i + 1, :] = row[:, 0:DH]
        buf[2 * i + 1:2 * i + 2, :] = row[:, DH:2 * DH]

    def get_row(value, i):
        return jnp.concatenate([value[2 * i:2 * i + 1], value[2 * i + 1:2 * i + 2]], axis=1)

    local[1].wait()
    local[2].wait()
    for i in range(HL):
        p = features(k_ref, i)
        pk[i] = p
        kb = p.astype(BF16)
        kf[i] = kb
        st[i] = dot_tn(kb, v_ref[:, head_cols(i)]).astype(BF16)
        put_row(zs, i, jnp.sum(kb.astype(F32), axis=0, keepdims=True))

    g4, m4 = ctx // 4, ctx % 4

    def member(d):
        return (m4 + d) % 4

    def l1_copy(src, dst, n, d):
        return rcopy(src.at[member(d)], dst.at[d], n + d, {"ctx": g4 * 4 + member(d)})

    def l2_copy(src, dst, n, d, sign):
        return rcopy(src, dst.at[d], n + 3 + d, {"ctx": (ctx + sign * 4 * d + NC) % NC})

    def l3_copy(src, dst, n, d):
        return rcopy(src.at[member(d)], dst.at[m4], n + 6 + d, {"ctx": g4 * 4 + member(d)})

    def group_has(d, sign):
        return g4 + d < 4 if sign > 0 else g4 >= d

    def l1_send(src, dst, n, h):
        for d in (1, 3, 2):
            @pl.when(member(d) // 2 == h)
            def _():
                l1_copy(src, dst, n, d).start()

    def l1_turn(src, buf, total, buf2, n, sign):
        buf[0] = src[m4]
        for d in (1, 3, 2):
            l1_copy(src, buf, n, d).wait_recv()
        total[...] = (buf[0].astype(F32) + buf[1].astype(F32)
                      + buf[2].astype(F32) + buf[3].astype(F32)).astype(BF16)
        for d in (1, 3, 2):
            @pl.when(group_has(d, sign))
            def _():
                l2_copy(total, buf2, n, d, sign).start()

    def l2_turn(buf, total, buf2, obuf, dst, n, sign):
        run[...] = jnp.zeros_like(run)
        for d in (1, 3, 2):
            @pl.when(group_has(d, -sign))
            def _():
                l2_copy(total, buf2, n, d, sign).wait_recv()
                run[...] += buf2[d].astype(F32)
        total_run = run[...]
        for c in (range(4) if sign > 0 else range(3, -1, -1)):
            obuf[c] = total_run.astype(BF16)
            total_run = total_run + buf[(m4 + 4 - c) % 4].astype(F32)
        for d in (1, 3, 2):
            l3_copy(obuf, dst, n, d).start()
        dst[m4] = obuf[m4]

    def l3_done(obuf, dst, n):
        for d in (1, 3, 2):
            l3_copy(obuf, dst, n, d).wait_recv()

    def scan_sent(src, buf, total, buf2, obuf, dst, n, sign):
        for d in (1, 2, 3):
            l1_copy(src, buf, n, d).wait_send()
            l3_copy(obuf, dst, n, d).wait_send()

            @pl.when(group_has(d, sign))
            def _():
                l2_copy(total, buf2, n, d, sign).wait_send()

    def row_copy(src, dst, n, d, sign):
        return rcopy(src, dst.at[d], n + d, {"ctx": (ctx + sign * d + NC) % NC})

    def each(count, fn):
        lax.fori_loop(1, count + 1, lambda d, _: (fn(d), 0)[1], 0)

    pl.semaphore_wait(barrier, 21)

    later, earlier = NC - 1 - ctx, ctx
    each(later, lambda d: row_copy(zs, zr, ZB, d, 1).start())
    l1_send(st, l1, D1, 0)
    l1_send(st, l1, D1, 1)

    ax = {}
    for k in (1, 3, 2):
        xx = (x + k) % 4
        ax[k] = rcopy(half(xx % 2), ogg.at[0, my_b, xl], AX + k, xdev(k))
        ax[k].start()

    def piece(n, k, side=0):
        yy, xx = (y + n) % 4, (x + 4 - k) % 4
        return ogg.at[side, yy * 2 + xx // 2, xx % 2]

    ayp, aym, ay2, ac = {}, {}, {}, {}

    def y_send(k):
        p = piece(0, k)
        src = half(xl) if k == 0 else p
        ayp[k] = rcopy(src, p, AYP + k, yp)
        aym[k] = rcopy(src, p, AYM + k, ym)
        ayp[k].start()
        aym[k].start()

    def a_got(n, k):
        p = piece(n, k)
        if n == 0:
            if k > 0:
                ax[k].wait_recv()
                y_send(k)
            else:
                local[4].wait()
        elif n == 2:
            ay2[k].wait_recv()
        else:
            (ayp if n == 3 else aym)[k].wait_recv()
            if (n == 3) == (k < 2):
                ay2[k] = rcopy(p, p, AY2 + k, yp if n == 3 else ym)
                ay2[k].start()
        c = rcopy(p, piece(n, k, 1), AC + 4 * n + k, sib)
        c.start()
        ac[n, k] = c

    y_send(0)

    bzp, bzm, bc = [], [], []

    def z_send(s, up):
        blk = (z + NZ - s) % NZ if up else (z + s) % NZ
        ref = owg.at[blk, rows_r]
        c = rcopy(ow_hbm.at[rows_r] if s == 0 else ref, ref,
                  (BZP if up else BZM) + s, zp if up else zm)
        c.start()
        (bzp if up else bzm).append(c)

    def b_recv(s, up):
        (bzp if up else bzm)[s].wait_recv()
        blk = (z + NZ - 1 - s) % NZ if up else (z + 1 + s) % NZ
        ref = owg.at[blk, rows_r]
        if s + 1 < (4 if up else 3):
            z_send(s + 1, up)
        c = rcopy(ref, ref, BC + (s if up else 4 + s), sib)
        c.start()
        bc.append(c)

    z_send(0, True)
    z_send(0, False)

    tri = (lax.broadcasted_iota(jnp.int32, (T, T), 0)
           >= lax.broadcasted_iota(jnp.int32, (T, T), 1))

    def q_phase(i):
        p = features(q_ref, i)
        pq[i] = p
        qb = p.astype(BF16)
        qf[i] = qb
        am = jnp.where(tri, dot_nt(qb, kf[i]), 0.0)
        rs[i] = jnp.sum(am, axis=-1, keepdims=True)
        amb = am.astype(BF16)
        ab[i] = amb
        nv[i] = dot_nn(amb, v_ref[:, head_cols(i)])

    atp = []
    ats = rcopy(at.at[pl.ds((1 - rep) * 2, 2)], atg.at[1, xl], ATS, sib)

    def attn_chunk(h):
        for i in (2 * h, 2 * h + 1):
            a = (nv[i] + dot_nn(qf[i], pr[i])) * rd[i]
            attn[i] = a
            at[i] = a.astype(BF16).T
        src = at.at[pl.ds(h * 2, 2)]
        c = rcopy(src, atg.at[(rep + h) % 2, xl], ATP + (rep + h) % 2, {"ctx": pair_ctx, "rep": h})
        c.start()
        atp.append(c)

        @pl.when(rep != h)
        def _():
            ats.start()

        @pl.when(rep == h)
        def _():
            atg[0, xl] = at[h * 2:h * 2 + 2]

    local[3].wait()
    q_phase(0)
    q_phase(1)
    a_got(0, 0)
    a_got(3, 0)
    a_got(0, 1)
    a_got(0, 3)
    q_phase(2)
    b_recv(0, True)
    b_recv(0, False)
    q_phase(3)
    l1_turn(st, l1, tot, l2, D1, 1)
    a_got(0, 2)

    each(earlier, lambda d: row_copy(zs, zr, ZB, d, 1).wait_recv())
    zsum = lax.fori_loop(1, ctx + 1, lambda d, a: a + zr[d], jnp.zeros((8, DH), F32))
    zpre[...] = zsum
    for i in range(HL):
        den = rs[i] + jnp.sum(qf[i].astype(F32) * get_row(zsum, i), axis=-1, keepdims=True)
        rd[i] = 1.0 / den

    b_recv(1, True)
    b_recv(1, False)
    l2_turn(l1, tot, l2, pf, pr, D1, 1)
    a_got(1, 0)
    a_got(3, 1)
    a_got(1, 3)
    b_recv(2, True)
    b_recv(2, False)
    l3_done(pf, pr, D1)
    attn_chunk(0)
    a_got(1, 2)
    a_got(1, 1)
    a_got(3, 3)
    b_recv(3, True)
    attn_chunk(1)
    local[5].wait()

    def go_part(mine):
        tok = xl if mine else 1 - xl

        def tile(m, _):
            rows = pl.ds(pl.multiple_of(m * 128, 128), 128)
            acc = dot_nt(ogg[0, 0, tok, rows, :], owg[0])
            for b in range(1, 8):
                acc += dot_nt(ogg[0, b, tok, rows, :], owg[b])
            if mine:
                gacc[rows, :] = acc
            else:
                gsend[rows, :] = acc.astype(BF16)
            return 0

        lax.fori_loop(0, 2, tile, 0)

    for c in bc:
        c.wait_recv()
    a_got(2, 1)
    a_got(2, 3)
    go_part(False)
    gx = rcopy(gsend, grecv, GX, pair)
    gx.start()

    a_got(3, 2)
    a_got(2, 0)
    a_got(2, 2)
    go_part(True)

    ats.wait_recv()
    for n in range(2):
        rcopy(atg.at[n, xl], atg.at[n, xl], ATP + n, pair).wait_recv()
    for c in ac.values():
        c.wait_recv()

    def w_block(b, ch):
        out = None
        for s in range(2):
            for t in range(2):
                d = dot_nn(atg[s, t, ch], ogg[s, b, t])
                out = d if out is None else out + d
        return out

    cp, cm = {}, {}

    def c_step(s, ch, up):
        sb, rb, cc = (cps, crp, cp) if up else (cms, crm, cm)
        val = w_block((z + 4 - s) % NZ if up else (z + 5 + s) % NZ, ch)
        if s > 0:
            cc[s - 1, ch].wait_recv()
            val += rb[s - 1, ch].astype(F32)
        sb[s, ch] = val.astype(BF16)
        c = rcopy(sb.at[s, ch], rb.at[s, ch], (CP if up else CM) + 2 * s + ch, zp if up else zm)
        c.start()
        cc[s, ch] = c

    def c_round(s):
        for ch in range(2):
            c_step(s, ch, True)
            if s < 3:
                c_step(s, ch, False)

    c_round(0)

    gx.wait_recv()

    def g_chunk(h):
        for i in (2 * h, 2 * h + 1):
            cols = head_cols(i)
            go = gacc[:, cols] + grecv[:, cols].astype(F32)
            r = rd[i]
            gb = (go * r).astype(BF16)
            gnb[i] = gb
            g = -jnp.sum(go * attn[i], axis=-1, keepdims=True) * r
            gd[i] = g
            qb = qf[i]
            st2[i] = dot_tn(qb, gb).astype(BF16)
            put_row(rs2, i, jnp.sum(qb.astype(F32) * g, axis=0, keepdims=True))
        l1_send(st2, l12, D2, h)

    g_chunk(0)
    g_chunk(1)
    each(earlier, lambda d: row_copy(rs2, rr2, RB, d, -1).start())

    def back(i, x_ref, w, out_ref):
        hi = w.astype(BF16)
        lo = (w - hi.astype(F32)).astype(BF16)
        t = dot_nn(hi, wc[i]) + dot_nn(lo, wc[i])
        u = t[:, 0:DH] + t[:, DH:2 * DH]
        xf = x_ref[:, head_cols(i)].astype(F32) * C
        out_ref[:, head_cols(i)] = (C * (u - xf * jnp.sum(w, axis=-1, keepdims=True))).astype(BF16)

    def dq_phase(i):
        gb, g, kb, qb = gnb[i], gd[i], kf[i], qf[i]
        bm = jnp.where(tri, dot_nt(gb, v_ref[:, head_cols(i)]) + g, 0.0).astype(BF16)
        dq = dot_nn(bm, kb) + dot_nt(gb, pr[i]) + g * get_row(zpre[...], i)
        back(i, q_ref, dq * pq[i], qg_ref)
        dk0[i] = dot_tn(bm, qb)
        dv0[i] = dot_tn(ab[i], gb)

    outs = []

    def out(src, dst):
        c = pltpu.make_async_copy(src, dst, lsem.at[6 + len(outs)])
        c.start()
        outs.append(c)

    dq_phase(0)
    c_round(1)
    l1_turn(st2, l12, tot2, l22, D2, -1)
    dq_phase(1)
    c_round(2)
    l2_turn(l12, tot2, l22, pf2, pr2, D2, -1)
    dq_phase(2)
    c_round(3)
    dq_phase(3)
    out(qg_ref, qg_hbm)

    each(later, lambda d: row_copy(rs2, rr2, RB, d, -1).wait_recv())
    rsum = lax.fori_loop(1, later + 1, lambda d, a: a + rr2[d], jnp.zeros((8, DH), F32))

    ccs = []

    def c_last(ch):
        own = w_block(z, ch)
        cp[3, ch].wait_recv()
        cm[2, ch].wait_recv()
        rows = pl.ds(pl.multiple_of(rep * 256 + ch * DH, DH), DH)
        wg_ref[ch] = (own + crp[3, ch].astype(F32) + crm[2, ch].astype(F32)).astype(BF16)
        c = rcopy(wg_ref.at[ch], wg_hbm.at[rows], CC + ch, sib)
        c.start()
        ccs.append(c)
        out(wg_ref.at[ch], wg_hbm.at[rows])

    def dk_chunk(h):
        for i in (2 * h, 2 * h + 1):
            s = pr2[i]
            vb = v_ref[:, head_cols(i)]
            dk = dk0[i] + dot_nt(vb, s) + get_row(rsum, i)
            back(i, k_ref, dk * pk[i], kg_ref)
            vg_ref[:, head_cols(i)] = (dv0[i] + dot_nn(kf[i], s)).astype(BF16)
        cols = slice(h * 256, h * 256 + 256)
        out(kg_ref.at[:, cols], kg_hbm.at[:, cols])
        out(vg_ref.at[:, cols], vg_hbm.at[:, cols])

    l3_done(pf2, pr2, D2)
    dk_chunk(0)
    c_last(0)
    c_last(1)
    dk_chunk(1)

    for group in (ax, ayp, aym, ay2, ac, cp, cm):
        for c in group.values():
            c.wait_send()
    for c in bzp + bzm + bc + atp + [ats, gx]:
        c.wait_send()
    scan_sent(st, l1, tot, l2, pf, pr, D1, 1)
    scan_sent(st2, l12, tot2, l22, pf2, pr2, D2, -1)
    each(later, lambda d: row_copy(zs, zr, ZB, d, 1).wait_send())
    each(earlier, lambda d: row_copy(rs2, rr2, RB, d, -1).wait_send())
    for c in ccs + outs:
        c.wait()


def store(*refs):
    ins, outs, bufs, sem = refs[0:4], refs[4:8], refs[8:12], refs[12]
    load = [pltpu.make_async_copy(a, b, sem.at[i]) for i, (a, b) in enumerate(zip(ins, bufs))]
    save = [pltpu.make_async_copy(a, b, sem.at[4 + i]) for i, (a, b) in enumerate(zip(bufs, outs))]
    for c in load:
        c.start()
    for c, d in zip(load, save):
        c.wait()
        d.start()
    for d in save:
        d.wait()


def on_device(queries, key_vecs, values, out_grad, out_weight, sign_bits):
    flat = lambda a: a.reshape(T, HL * DH)
    hbm = pl.BlockSpec(memory_space=pltpu.HBM)
    state = pltpu.VMEM((HL, M, DH), BF16)
    total = pltpu.VMEM((M, DH), BF16)
    row = pltpu.VMEM((8, DH), F32)
    rows = pltpu.VMEM((NC, 8, DH), F32)
    heads = lambda n, dt: pltpu.VMEM((HL, T, n), dt)
    blocks = lambda n: pltpu.VMEM((n, 2, DH, 256), BF16)
    act = pltpu.VMEM((T, HL * DH), BF16)
    shapes = [jax.ShapeDtypeStruct((T, HL * DH), BF16)] * 3 + [jax.ShapeDtypeStruct((HL * DH, 256), BF16)]
    grads = pl.pallas_call(
        kernel,
        out_shape=shapes,
        in_specs=[hbm] * 6,
        out_specs=[hbm] * 4,
        scratch_shapes=[
            act, act, act, pltpu.VMEM((3, HL, M), jnp.int32),
            act, act, act, pltpu.VMEM((2, DH, 256), BF16),
            pltpu.VMEM((2, 8, 2, T, 256), BF16),
            pltpu.VMEM((NZ, 512, 256), BF16),
            pltpu.VMEM((T, 512), F32),
            act, act,
            state, state, state, total, state, state,
            state, state, state, total, state, state, pltpu.VMEM((M, DH), F32),
            row, rows, row, rows, row,
            heads(256, BF16),
            heads(M, F32), heads(M, F32), heads(M, BF16), heads(M, BF16),
            heads(T, BF16), heads(DH, F32), heads(1, F32), heads(1, F32),
            heads(DH, F32),
            pltpu.VMEM((HL, DH, T), BF16),
            pltpu.VMEM((2, 2, 2, DH, T), BF16),
            heads(DH, BF16), heads(1, F32), heads(M, F32), heads(DH, F32),
            blocks(4), blocks(3), blocks(4), blocks(3),
            pltpu.SemaphoreType.DMA((NSEM,)),
            pltpu.SemaphoreType.DMA((NSEM,)),
            pltpu.SemaphoreType.DMA((13,)),
        ],
        compiler_params=pltpu.CompilerParams(
            collective_id=0, has_side_effects=True, vmem_limit_bytes=62 * 1024 * 1024),
        cost_estimate=pl.CostEstimate(
            flops=5 * 10**9, bytes_accessed=4 * 10**6, transcendentals=5 * 10**5),
        name="performer_back",
    )(flat(queries), flat(key_vecs), flat(values), flat(out_grad), out_weight, sign_bits.transpose(1, 0, 2))
    qg, kg, vg, wg = pl.pallas_call(
        store,
        out_shape=shapes,
        in_specs=[hbm] * 4,
        out_specs=[hbm] * 4,
        scratch_shapes=[act, act, act, pltpu.VMEM((HL * DH, 256), BF16), pltpu.SemaphoreType.DMA((8,))],
        compiler_params=pltpu.CompilerParams(vmem_limit_bytes=62 * 1024 * 1024),
        name="store",
    )(*grads)
    shaped = lambda a: a.reshape(1, T, HL * DH)
    return shaped(qg), shaped(kg), shaped(vg), wg


def solution(mesh):
    tok = P("rep", "ctx", "head")
    return jax.shard_map(
        on_device, mesh=mesh,
        in_specs=(tok, tok, tok, tok, P("head", "ctx"), P("head", None, None)),
        out_specs=(tok, tok, tok, P("head", "ctx")),
        check_vma=False,
    )
```

time: 80.8 us -> 74.5 us (0.922)
  Pallas kernels: 78.5 us -> 73.7 us
  local copies, waits for them, and re-layouts: 1.32 us -> 0 us
    pallas_call x2, Pallas kernels: 78.5 us -> 73.7 us  [the longest x1 71.7 us: on_device(): pl.pallas_call(kernel, out_shape=shapes, in_specs=[hbm] * 6, out_specs=[h...]
    unnamed x1 -> x0, local copies, waits for them, and re-layouts: 1.32 us -> none
where the time goes in v3:
time: 74.5 us; the launch traced here: 74.3 us
  Pallas kernels  73.7 us (99%)
    pallas_call x1, Pallas kernels, on_device(): pl.pallas_call(kernel, out_shape=shapes, in_specs=[hbm] * 6, out_specs=[h...  71.7 us
    pallas_call x1, Pallas kernels, on_device(): pl.pallas_call(store, out_shape=shapes, in_specs=[hbm] * 4, out_specs=[hb...  1.98 us

profile of v3, /device:TPU:1, one launch (start us, length us, event | category | flops | bytes accessed | tf_op | source)
XLA Modules:
  0.0 74.3 jit_solution(4538314506005890608)
XLA Ops:
  0.6 71.7 %performer_back.1 = (bf16[256,512]{1,0:T(8,128)(2,1)}, bf16[256,512]{1,0:T(8,128)(2,1)}, bf16[256,512]{1,0:T(8,128)(2,1)}, bf16[512,256]{1,0:T(8,128)(2,1)}) custom-call(bf16[256,512]{1,0:T(8,128)(2,1)} %bitcast.8, bf16[256,512]{1,0:T(8,128)(2,1)} %bitcast.9, bf16[256,512]{1,0:T(8,128)(2,1)} %bitcast.10, bf16[256,512]{1,0:T(8,128)(2,1)} %bitcast.11, ...), custom_call_target="tpu_custom_call" | custom-call | flops 5000000000 | bytes 4000000 | tf_op jit(solution)/shard_map/performer_back/pallas_call | solution.py:556
  72.4 2.0 %store.1 = (bf16[256,512]{1,0:T(8,128)(2,1)}, bf16[256,512]{1,0:T(8,128)(2,1)}, bf16[256,512]{1,0:T(8,128)(2,1)}, bf16[512,256]{1,0:T(8,128)(2,1)}) custom-call(bf16[256,512]{1,0:T(8,128)(2,1)} %get-tuple-element.12.refs_0_, bf16[256,512]{1,0:T(8,128)(2,1)} %get-tuple-element.13.refs_1_, bf16[256,512]{1,0:T(8,128)(2,1)} %get-tuple-element.14.refs_2_, ...), custom_call_target="tpu_custom_call" | custom-call | tf_op jit(solution)/shard_map/store/pallas_call | solution.py:589

commit v4 on v3

--- a/solution.py
+++ b/solution.py
@@ -59,7 +59,7 @@
            ogg, owg, gacc, gsend, grecv,
            st, l1, l2, tot, pf, pr, st2, l12, l22, tot2, pf2, pr2, run, zs, zr, rs2, rr2, zpre,
            wc, pq, pk, qf, kf, ab, nv, rs, rd, attn, at, atg,
-           gnb, gd, dk0, dv0, cps, cms, crp, crm,
+           gnb, gd, dk0, dv0, wpre, cps, cms, crp, crm,
            ssem, rsem, lsem):
     ctx = lax.axis_index("ctx")
     head = lax.axis_index("head")
@@ -225,8 +225,6 @@
 
     later, earlier = NC - 1 - ctx, ctx
     each(later, lambda d: row_copy(zs, zr, ZB, d, 1).start())
-    l1_send(st, l1, D1, 0)
-    l1_send(st, l1, D1, 1)
 
     ax = {}
     for k in (1, 3, 2):
@@ -291,6 +289,8 @@
 
     z_send(0, True)
     z_send(0, False)
+    l1_send(st, l1, D1, 0)
+    l1_send(st, l1, D1, 1)
 
     tri = (lax.broadcasted_iota(jnp.int32, (T, T), 0)
            >= lax.broadcasted_iota(jnp.int32, (T, T), 1))
@@ -334,12 +334,14 @@
     a_got(3, 0)
     a_got(0, 1)
     a_got(0, 3)
-    q_phase(2)
     b_recv(0, True)
     b_recv(0, False)
+    q_phase(2)
+    l1_turn(st, l1, tot, l2, D1, 1)
+    b_recv(1, True)
+    b_recv(1, False)
+    a_got(0, 2)
     q_phase(3)
-    l1_turn(st, l1, tot, l2, D1, 1)
-    a_got(0, 2)
 
     each(earlier, lambda d: row_copy(zs, zr, ZB, d, 1).wait_recv())
     zsum = lax.fori_loop(1, ctx + 1, lambda d, a: a + zr[d], jnp.zeros((8, DH), F32))
@@ -348,11 +350,9 @@
         den = rs[i] + jnp.sum(qf[i].astype(F32) * get_row(zsum, i), axis=-1, keepdims=True)
         rd[i] = 1.0 / den
 
-    b_recv(1, True)
-    b_recv(1, False)
-    l2_turn(l1, tot, l2, pf, pr, D1, 1)
     a_got(1, 0)
     a_got(3, 1)
+    l2_turn(l1, tot, l2, pf, pr, D1, 1)
     a_got(1, 3)
     b_recv(2, True)
     b_recv(2, False)
@@ -392,8 +392,6 @@
     a_got(3, 2)
     a_got(2, 0)
     a_got(2, 2)
-    go_part(True)
-
     ats.wait_recv()
     for n in range(2):
         rcopy(atg.at[n, xl], atg.at[n, xl], ATP + n, pair).wait_recv()
@@ -410,10 +408,21 @@
 
     cp, cm = {}, {}
 
+    def c_ready(s):
+        for ch in range(2):
+            if s < 4:
+                wpre[0, ch] = w_block((z + 4 - s) % NZ, ch)
+                if s < 3:
+                    wpre[1, ch] = w_block((z + 5 + s) % NZ, ch)
+            else:
+                wpre[0, ch] = w_block(z, ch)
+
     def c_step(s, ch, up):
         sb, rb, cc = (cps, crp, cp) if up else (cms, crm, cm)
-        val = w_block((z + 4 - s) % NZ if up else (z + 5 + s) % NZ, ch)
-        if s > 0:
+        if s == 0:
+            val = w_block((z + 4) % NZ if up else (z + 5) % NZ, ch)
+        else:
+            val = wpre[0 if up else 1, ch]
             cc[s - 1, ch].wait_recv()
             val += rb[s - 1, ch].astype(F32)
         sb[s, ch] = val.astype(BF16)
@@ -428,6 +437,8 @@
                 c_step(s, ch, False)
 
     c_round(0)
+    go_part(True)
+    c_ready(1)
 
     gx.wait_recv()
 
@@ -472,14 +483,17 @@
         c.start()
         outs.append(c)
 
+    c_round(1)
+    c_ready(2)
     dq_phase(0)
-    c_round(1)
     l1_turn(st2, l12, tot2, l22, D2, -1)
+    c_round(2)
+    c_ready(3)
     dq_phase(1)
-    c_round(2)
     l2_turn(l12, tot2, l22, pf2, pr2, D2, -1)
+    c_round(3)
+    c_ready(4)
     dq_phase(2)
-    c_round(3)
     dq_phase(3)
     out(qg_ref, qg_hbm)
 
@@ -489,7 +503,7 @@
     ccs = []
 
     def c_last(ch):
-        own = w_block(z, ch)
+        own = wpre[0, ch]
         cp[3, ch].wait_recv()
         cm[2, ch].wait_recv()
         rows = pl.ds(pl.multiple_of(rep * 256 + ch * DH, DH), DH)
@@ -575,7 +589,7 @@
             pltpu.VMEM((HL, DH, T), BF16),
             pltpu.VMEM((2, 2, 2, DH, T), BF16),
             heads(DH, BF16), heads(1, F32), heads(M, F32), heads(DH, F32),
-            blocks(4), blocks(3), blocks(4), blocks(3),
+            pltpu.VMEM((2, 2, DH, 256), F32), blocks(4), blocks(3), blocks(4), blocks(3),
             pltpu.SemaphoreType.DMA((NSEM,)),
             pltpu.SemaphoreType.DMA((NSEM,)),
             pltpu.SemaphoreType.DMA((13,)),

time: 74.5 us -> 72.9 us (0.979)
  Pallas kernels: 73.7 us -> 72.1 us
    pallas_call x1, Pallas kernels: 71.7 us -> 70.2 us  [on_device(): pl.pallas_call(kernel, out_shape=shapes, in_specs=[hbm] * 6, out_specs=[h...]
where the time goes in v4:
time: 72.9 us; the launch traced here: 72.8 us
  Pallas kernels  72.1 us (99%)
    pallas_call x1, Pallas kernels, on_device(): pl.pallas_call(kernel, out_shape=shapes, in_specs=[hbm] * 6, out_specs=[h...  70.2 us
    pallas_call x1, Pallas kernels, on_device(): pl.pallas_call(store, out_shape=shapes, in_specs=[hbm] * 4, out_specs=[hb...  1.98 us

profile of v4, /device:TPU:1, one launch (start us, length us, event | category | flops | bytes accessed | tf_op | source)
XLA Modules:
  0.0 72.8 jit_solution(10699352818922796237)
XLA Ops:
  0.6 70.2 %performer_back.1 = (bf16[256,512]{1,0:T(8,128)(2,1)}, bf16[256,512]{1,0:T(8,128)(2,1)}, bf16[256,512]{1,0:T(8,128)(2,1)}, bf16[512,256]{1,0:T(8,128)(2,1)}) custom-call(bf16[256,512]{1,0:T(8,128)(2,1)} %bitcast.8, bf16[256,512]{1,0:T(8,128)(2,1)} %bitcast.9, bf16[256,512]{1,0:T(8,128)(2,1)} %bitcast.10, bf16[256,512]{1,0:T(8,128)(2,1)} %bitcast.11, ...), custom_call_target="tpu_custom_call" | custom-call | flops 5000000000 | bytes 4000000 | tf_op jit(solution)/shard_map/performer_back/pallas_call | solution.py:570
  70.8 2.0 %store.1 = (bf16[256,512]{1,0:T(8,128)(2,1)}, bf16[256,512]{1,0:T(8,128)(2,1)}, bf16[256,512]{1,0:T(8,128)(2,1)}, bf16[512,256]{1,0:T(8,128)(2,1)}) custom-call(bf16[256,512]{1,0:T(8,128)(2,1)} %get-tuple-element.12.refs_0_, bf16[256,512]{1,0:T(8,128)(2,1)} %get-tuple-element.13.refs_1_, bf16[256,512]{1,0:T(8,128)(2,1)} %get-tuple-element.14.refs_2_, ...), custom_call_target="tpu_custom_call" | custom-call | tf_op jit(solution)/shard_map/store/pallas_call | solution.py:603

commit v5 on v4

--- a/solution.py
+++ b/solution.py
@@ -19,12 +19,12 @@
 MESH = pl.DeviceIdType.MESH
 
 AX, AYP, AYM, AY2, AC = 0, 4, 8, 12, 16
-BZP, BZM, BC = 32, 36, 39
+BZP, BZM, BC = 114, 122, 128
 GX, ATS, ATP = 46, 47, 48
 CP, CM, CC = 50, 58, 64
 D1, D2 = 65, 74
 ZB, RB = 83, 98
-NSEM = 114
+NSEM = 142
 
 
 def dot_nn(a, b):
@@ -105,7 +105,6 @@
         return og_hbm.at[:, pl.ds(pl.multiple_of(s * 256, 256), 256)]
 
     my_b = head
-    rows_r = pl.ds(pl.multiple_of(rep * 256, 256), 256)
     local = [pltpu.make_async_copy(a, b, lsem.at[n]) for n, (a, b) in enumerate((
         (sb_hbm, sb_ref), (k_hbm, k_ref), (v_hbm, v_ref), (q_hbm, q_ref),
         (half(xl), ogg.at[0, my_b, xl]), (ow_hbm, owg.at[z])))]
@@ -267,25 +266,30 @@
 
     y_send(0)
 
-    bzp, bzm, bc = [], [], []
-
-    def z_send(s, up):
+    bzp, bzm, bc = {}, {}, []
+
+    def z_rows(h):
+        return pl.ds(pl.multiple_of(rep * 256 + h * 128, 128), 128)
+
+    def z_send(s, up, pieces=(0, 1)):
         blk = (z + NZ - s) % NZ if up else (z + s) % NZ
-        ref = owg.at[blk, rows_r]
-        c = rcopy(ow_hbm.at[rows_r] if s == 0 else ref, ref,
-                  (BZP if up else BZM) + s, zp if up else zm)
-        c.start()
-        (bzp if up else bzm).append(c)
+        for h in pieces:
+            ref = owg.at[blk, z_rows(h)]
+            c = rcopy(ow_hbm.at[z_rows(h)] if s == 0 else ref, ref,
+                      (BZP if up else BZM) + 2 * s + h, zp if up else zm)
+            c.start()
+            (bzp if up else bzm)[s, h] = c
 
     def b_recv(s, up):
-        (bzp if up else bzm)[s].wait_recv()
         blk = (z + NZ - 1 - s) % NZ if up else (z + 1 + s) % NZ
-        ref = owg.at[blk, rows_r]
-        if s + 1 < (4 if up else 3):
-            z_send(s + 1, up)
-        c = rcopy(ref, ref, BC + (s if up else 4 + s), sib)
-        c.start()
-        bc.append(c)
+        for h in range(2):
+            (bzp if up else bzm)[s, h].wait_recv()
+            if s + 1 < (4 if up else 3):
+                z_send(s + 1, up, (h,))
+            ref = owg.at[blk, z_rows(h)]
+            c = rcopy(ref, ref, BC + 2 * (s if up else 4 + s) + h, sib)
+            c.start()
+            bc.append(c)
 
     z_send(0, True)
     z_send(0, False)
@@ -530,10 +534,10 @@
     c_last(1)
     dk_chunk(1)
 
-    for group in (ax, ayp, aym, ay2, ac, cp, cm):
+    for group in (ax, ayp, aym, ay2, ac, cp, cm, bzp, bzm):
         for c in group.values():
             c.wait_send()
-    for c in bzp + bzm + bc + atp + [ats, gx]:
+    for c in bc + atp + [ats, gx]:
         c.wait_send()
     scan_sent(st, l1, tot, l2, pf, pr, D1, 1)
     scan_sent(st2, l12, tot2, l22, pf2, pr2, D2, -1)

time: 72.9 us -> 73.3 us (level)
  no operation moved by 1% of the time
where the time goes in v5:
time: 73.3 us; the launch traced here: 73.2 us
  Pallas kernels  72.5 us (99%)
    pallas_call x1, Pallas kernels, on_device(): pl.pallas_call(kernel, out_shape=shapes, in_specs=[hbm] * 6, out_specs=[h...  70.6 us
    pallas_call x1, Pallas kernels, on_device(): pl.pallas_call(store, out_shape=shapes, in_specs=[hbm] * 4, out_specs=[hb...  1.98 us

profile of v5, /device:TPU:1, one launch (start us, length us, event | category | flops | bytes accessed | tf_op | source)
XLA Modules:
  0.0 73.2 jit_solution(1167632367718065653)
XLA Ops:
  0.6 70.6 %performer_back.1 = (bf16[256,512]{1,0:T(8,128)(2,1)}, bf16[256,512]{1,0:T(8,128)(2,1)}, bf16[256,512]{1,0:T(8,128)(2,1)}, bf16[512,256]{1,0:T(8,128)(2,1)}) custom-call(bf16[256,512]{1,0:T(8,128)(2,1)} %bitcast.8, bf16[256,512]{1,0:T(8,128)(2,1)} %bitcast.9, bf16[256,512]{1,0:T(8,128)(2,1)} %bitcast.10, bf16[256,512]{1,0:T(8,128)(2,1)} %bitcast.11, ...), custom_call_target="tpu_custom_call" | custom-call | flops 5000000000 | bytes 4000000 | tf_op jit(solution)/shard_map/performer_back/pallas_call | solution.py:574
  71.2 2.0 %store.1 = (bf16[256,512]{1,0:T(8,128)(2,1)}, bf16[256,512]{1,0:T(8,128)(2,1)}, bf16[256,512]{1,0:T(8,128)(2,1)}, bf16[512,256]{1,0:T(8,128)(2,1)}) custom-call(bf16[256,512]{1,0:T(8,128)(2,1)} %get-tuple-element.12.refs_0_, bf16[256,512]{1,0:T(8,128)(2,1)} %get-tuple-element.13.refs_1_, bf16[256,512]{1,0:T(8,128)(2,1)} %get-tuple-element.14.refs_2_, ...), custom_call_target="tpu_custom_call" | custom-call | tf_op jit(solution)/shard_map/store/pallas_call | solution.py:607
